TPU v7x, 32 devices: a whole 2x2x4 slice. The times are simulated.
32 devices in a mesh: shard: 4 (over x, core), heads: 4 (over z), tensor: 2 (over y).
Axes of the slice: x: 2, y: 2, z: 4, core: 2. Of those that a mesh axis runs over, the one named last changes fastest.
Arguments:
- tokens: bfloat16 [64, 197, 768], P(('shard', 'tensor')), may hold values from -6 to 6
- norm_scales: bfloat16 [2, 768], P(None, ('shard', 'tensor')), may hold values from 0.5 to 1.5
- norm_biases: bfloat16 [2, 768], P(None, ('shard', 'tensor')), may hold values from -0.59765625 to 0.59765625
- w_attn: bfloat16 [4, 768, 768], P(None, ('shard', 'tensor'), 'heads'), may hold values from -0.3125 to 0.3125
- phi: bfloat16 [768, 64], P(('shard', 'tensor'), 'heads'), may hold values from -0.109375 to 0.109375
- experts: bfloat16 [768, 2, 64, 3072], P('shard', None, 'heads', 'tensor'), may hold values from -2 to 2
- in_bias: bfloat16 [64, 3072], P('heads', ('shard', 'tensor')), may hold values from -0.59765625 to 0.59765625
- out_bias: bfloat16 [64, 768], P('heads', ('shard', 'tensor')), may hold values from -4.78125 to 4.78125
- cotangent: bfloat16 [64, 197, 768], P(('shard', 'tensor')), may hold values from -6 to 6
Outputs:
- output: bfloat16 [64, 197, 768], P(('shard', 'tensor'))
- input_grad: bfloat16 [64, 197, 768], P(('shard', 'tensor'))
- scales_grad: float32 [2, 768], P(None, ('shard', 'tensor'))
- biases_grad: float32 [2, 768], P(None, ('shard', 'tensor'))
- attn_grad: float32 [4, 768, 768], P(None, ('shard', 'tensor'), 'heads')
- phi_grad: float32 [768, 64], P(('shard', 'tensor'), 'heads')
- experts_grad: float32 [768, 2, 64, 3072], P('shard', None, 'heads', 'tensor')
- in_bias_grad: float32 [64, 3072], P('heads', ('shard', 'tensor'))
- out_bias_grad: float32 [64, 768], P('heads', ('shard', 'tensor'))
All inputs are finite; a program needn't handle non-finite values.
Results may differ from a plain program's by a relative error of at most 0.019.
Values may be sent and summed in bfloat16 or wider, within the bound.
A program may use at most 576 MiB of HBM per device.

v0:
```python
from functools import partial

import jax
import jax.numpy as jnp
from jax import lax
from jax.sharding import PartitionSpec as P

HEAD_DIM = 64


epsilon = 1e-06


def joined(value, axis, combine):
    everything = jax.tree.map(lambda part: lax.all_gather(part, axis), value)
    first = jax.tree.map(lambda part: part[0], everything)

    def lap(k, so_far):
        return combine(so_far, jax.tree.map(lambda part: part[k], everything))

    return lax.fori_loop(1, lax.axis_size(axis), lap, first)


def normalize(values, scale, shift):
    centered = values - jnp.mean(values, axis=-1, keepdims=True)
    variance = jnp.mean(centered * centered, axis=-1, keepdims=True)
    inverse = lax.rsqrt(variance + epsilon)
    unit_part = centered * inverse
    return (unit_part * scale + shift, unit_part, inverse)


def normalize_back(grad_output, unit_part, inverse, scale):
    scaled = grad_output * scale
    average = jnp.mean(scaled, axis=-1, keepdims=True)
    projection = jnp.mean(scaled * unit_part, axis=-1, keepdims=True)
    grad_input = inverse * (scaled - average - unit_part * projection)
    return (
        grad_input,
        jnp.sum(grad_output * unit_part, axis=(0, 1)),
        jnp.sum(grad_output, axis=(0, 1)),
    )


def fetch_experts(experts):
    return lax.all_gather(experts, "shard", axis=0, tiled=True)


def merge_stats(earlier, later):
    highest_value = jnp.maximum(earlier[0], later[0])
    return (
        highest_value,
        earlier[1] * jnp.exp(earlier[0] - highest_value)
        + later[1] * jnp.exp(later[0] - highest_value),
    )


def shards(tokens, norm_scales, norm_biases, w_attn, phi, experts, in_bias, out_bias, cotangent):
    shard_rows = tokens.shape[0]
    seq_len = tokens.shape[1]
    tensor_index = lax.axis_index("tensor")
    scales, biases, attn_full, phi_full, in_full, out_full = (
        lax.all_gather(norm_scales, ("shard", "tensor"), axis=1, tiled=True),
        lax.all_gather(norm_biases, ("shard", "tensor"), axis=1, tiled=True),
        lax.all_gather(w_attn, ("shard", "tensor"), axis=1, tiled=True),
        lax.all_gather(phi, ("shard", "tensor"), axis=0, tiled=True),
        lax.all_gather(in_bias, ("shard", "tensor"), axis=1, tiled=True),
        lax.all_gather(out_bias, ("shard", "tensor"), axis=1, tiled=True),
    )
    scales = scales.astype(jnp.float32)
    biases = biases.astype(jnp.float32)
    in_full = in_full.astype(jnp.float32)
    out_full = out_full.astype(jnp.float32)
    local_width = attn_full.shape[2]
    local_heads = local_width // HEAD_DIM
    factor = HEAD_DIM ** (-0.5)
    expert_full = fetch_experts(experts)
    hidden_local = expert_full.shape[3]
    in_local = lax.dynamic_slice_in_dim(in_full, tensor_index * hidden_local, hidden_local, 1)
    inputs = tokens.astype(jnp.float32)
    normed_one, unit_one, inverse_one = normalize(inputs, scales[0], biases[0])
    normed_one_b = normed_one.astype(jnp.bfloat16)
    projected = jnp.einsum(
        "nsd,kdc->knsc", normed_one_b, attn_full[:3], preferred_element_type=jnp.float32
    ).astype(jnp.bfloat16)
    query, keyed, valued = projected.reshape(3, shard_rows, seq_len, local_heads, HEAD_DIM)
    scores = (
        jnp.einsum("nqhe,nkhe->nhqk", query, keyed, preferred_element_type=jnp.float32) * factor
    )
    score_peak = jnp.max(scores, axis=-1, keepdims=True)
    exponent = jnp.exp(scores - score_peak)
    row_total = jnp.sum(exponent, axis=-1, keepdims=True)
    logsum = score_peak + jnp.log(row_total)
    probs_b = (exponent / row_total).astype(jnp.bfloat16)
    context = jnp.einsum("nhqk,nkhe->nqhe", probs_b, valued, preferred_element_type=jnp.float32)
    context_b = context.astype(jnp.bfloat16).reshape(shard_rows, seq_len, local_width)
    attn_part = jnp.einsum(
        "nsc,dc->nsd", context_b, attn_full[3], preferred_element_type=jnp.float32
    )
    attended = lax.psum(attn_part, "heads")
    hidden_one = inputs + attended
    normed_two, unit_two, inverse_two = normalize(hidden_one, scales[1], biases[1])
    normed_two_b = normed_two.astype(jnp.bfloat16)
    paired = lax.all_gather(normed_two_b, "tensor", axis=0, tiled=True)
    logits = jnp.einsum("nsd,de->nse", paired, phi_full, preferred_element_type=jnp.float32)
    dispatch = jax.nn.softmax(logits, axis=1)
    dispatch_b = dispatch.astype(jnp.bfloat16)
    slot_in = jnp.einsum(
        "nse,nsd->ned", dispatch_b, paired, preferred_element_type=jnp.float32
    ).astype(jnp.bfloat16)
    pre_act = (
        jnp.einsum("ned,def->nef", slot_in, expert_full[:, 0], preferred_element_type=jnp.float32)
        + in_local
    )
    activated_b = jax.nn.gelu(pre_act, approximate=False).astype(jnp.bfloat16)
    out_part = jnp.einsum(
        "nef,def->ned", activated_b, expert_full[:, 1], preferred_element_type=jnp.float32
    )
    slot_out = lax.psum_scatter(out_part, "tensor", scatter_dimension=0, tiled=True) + out_full
    slot_out_b = slot_out.astype(jnp.bfloat16)
    own_logits = lax.dynamic_slice_in_dim(logits, tensor_index * shard_rows, shard_rows, 0)
    row_peak = jnp.max(own_logits, axis=-1)
    row_sum = jnp.sum(jnp.exp(own_logits - row_peak[..., None]), axis=-1)
    peak_all, total_all = joined((row_peak, row_sum), "heads", merge_stats)
    combine = jnp.exp(own_logits - peak_all[..., None]) / total_all[..., None]
    combine_b = combine.astype(jnp.bfloat16)
    mixed_part = jnp.einsum(
        "nse,ned->nsd", combine_b, slot_out_b, preferred_element_type=jnp.float32
    )
    mixed = lax.psum(mixed_part, "heads")
    output = (hidden_one + mixed).astype(jnp.bfloat16)
    grad_out = cotangent.astype(jnp.float32)
    grad_combine = jnp.einsum(
        "nsd,ned->nse", cotangent, slot_out_b, preferred_element_type=jnp.float32
    )
    grad_slot = jnp.einsum(
        "nse,nsd->ned", combine_b, cotangent, preferred_element_type=jnp.float32
    ).astype(jnp.bfloat16)
    weighted_part = jnp.sum(combine * grad_combine, axis=-1)
    weighted = lax.psum(weighted_part, "heads")
    grad_comb_logits = combine * (grad_combine - weighted[..., None])
    expert_back = fetch_experts(experts)
    grad_slot_pair = lax.all_gather(grad_slot, "tensor", axis=0, tiled=True)
    grad_act = jnp.einsum(
        "ned,def->nef", grad_slot_pair, expert_back[:, 1], preferred_element_type=jnp.float32
    )
    gelu_value, gelu_back = jax.vjp(partial(jax.nn.gelu, approximate=False), pre_act)
    grad_pre = gelu_back(grad_act)[0].astype(jnp.bfloat16)
    grad_slot_in = jnp.einsum(
        "nef,def->ned", grad_pre, expert_back[:, 0], preferred_element_type=jnp.float32
    ).astype(jnp.bfloat16)
    input_term = jnp.einsum("ned,nef->def", slot_in, grad_pre, preferred_element_type=jnp.float32)
    output_term = jnp.einsum(
        "ned,nef->def", grad_slot_pair, activated_b, preferred_element_type=jnp.float32
    )
    experts_grad = lax.psum_scatter(
        jnp.stack((input_term, output_term), axis=1), "shard", scatter_dimension=0, tiled=True
    )
    grad_dispatch = jnp.einsum(
        "nsd,ned->nse", paired, grad_slot_in, preferred_element_type=jnp.float32
    )
    grad_disp_logits = dispatch * (
        grad_dispatch - jnp.sum(dispatch * grad_dispatch, axis=1, keepdims=True)
    )
    grad_tokens_pair = jnp.einsum(
        "nse,ned->nsd", dispatch_b, grad_slot_in, preferred_element_type=jnp.float32
    )
    grad_tokens, grad_disp_own = (
        lax.psum_scatter(grad_tokens_pair, "tensor", scatter_dimension=0, tiled=True),
        lax.psum_scatter(grad_disp_logits, "tensor", scatter_dimension=0, tiled=True),
    )
    grad_logits = (grad_disp_own + grad_comb_logits).astype(jnp.bfloat16)
    grad_tokens = grad_tokens + jnp.einsum(
        "nse,de->nsd", grad_logits, phi_full, preferred_element_type=jnp.float32
    )
    phi_grad = jnp.einsum(
        "nsd,nse->de", normed_two_b, grad_logits, preferred_element_type=jnp.float32
    )
    grad_normed_two = lax.psum(grad_tokens, "heads")
    grad_hidden_norm, scale_two_grad, bias_two_grad = normalize_back(
        grad_normed_two, unit_two, inverse_two, scales[1]
    )
    grad_hidden = grad_out + grad_hidden_norm
    grad_hidden_b = grad_hidden.astype(jnp.bfloat16)
    out_weight_grad = jnp.einsum(
        "nsd,nsc->dc", grad_hidden_b, context_b, preferred_element_type=jnp.float32
    )
    grad_context = jnp.einsum(
        "nsd,dc->nsc", grad_hidden_b, attn_full[3], preferred_element_type=jnp.float32
    ).astype(jnp.bfloat16)
    grad_context = grad_context.reshape(shard_rows, seq_len, local_heads, HEAD_DIM)
    probs_again = jnp.exp(
        jnp.einsum("nqhe,nkhe->nhqk", query, keyed, preferred_element_type=jnp.float32) * factor
        - logsum
    )
    grad_value = jnp.einsum(
        "nhqk,nqhe->nkhe",
        probs_again.astype(jnp.bfloat16),
        grad_context,
        preferred_element_type=jnp.float32,
    ).astype(jnp.bfloat16)
    grad_probs = jnp.einsum(
        "nqhe,nkhe->nhqk", grad_context, valued, preferred_element_type=jnp.float32
    )
    grad_scores = (
        probs_again * (grad_probs - jnp.sum(probs_again * grad_probs, axis=-1, keepdims=True))
    ).astype(jnp.bfloat16)
    grad_query = (
        jnp.einsum("nhqk,nkhe->nqhe", grad_scores, keyed, preferred_element_type=jnp.float32)
        * factor
    ).astype(jnp.bfloat16)
    grad_key = (
        jnp.einsum("nhqk,nqhe->nkhe", grad_scores, query, preferred_element_type=jnp.float32)
        * factor
    ).astype(jnp.bfloat16)
    grad_proj = jnp.stack((grad_query, grad_key, grad_value)).reshape(
        3, shard_rows, seq_len, local_width
    )
    proj_grad = jnp.einsum(
        "nsd,knsc->kdc", normed_one_b, grad_proj, preferred_element_type=jnp.float32
    )
    grad_normed_part = jnp.einsum(
        "knsc,kdc->nsd", grad_proj, attn_full[:3], preferred_element_type=jnp.float32
    )
    grad_normed_one = lax.psum(grad_normed_part, "heads")
    grad_input_norm, scale_one_grad, bias_one_grad = normalize_back(
        grad_normed_one, unit_one, inverse_one, scales[0]
    )
    input_grad = (grad_hidden + grad_input_norm).astype(jnp.bfloat16)
    in_grad_half = jnp.sum(grad_pre.astype(jnp.float32), axis=0)
    in_grad_full = lax.dynamic_update_slice_in_dim(
        jnp.zeros(in_full.shape, jnp.float32), in_grad_half, tensor_index * hidden_local, 1
    )
    out_grad = jnp.sum(grad_slot.astype(jnp.float32), axis=0)
    attn_grad = jnp.concatenate((proj_grad, out_weight_grad[None]), axis=0)
    reduced = (
        lax.psum_scatter(
            jnp.stack((scale_one_grad, scale_two_grad)),
            ("shard", "tensor"),
            scatter_dimension=1,
            tiled=True,
        ),
        lax.psum_scatter(
            jnp.stack((bias_one_grad, bias_two_grad)),
            ("shard", "tensor"),
            scatter_dimension=1,
            tiled=True,
        ),
        lax.psum_scatter(attn_grad, ("shard", "tensor"), scatter_dimension=1, tiled=True),
        lax.psum_scatter(phi_grad, ("shard", "tensor"), scatter_dimension=0, tiled=True),
        lax.psum_scatter(in_grad_full, ("shard", "tensor"), scatter_dimension=1, tiled=True),
        lax.psum_scatter(out_grad, ("shard", "tensor"), scatter_dimension=1, tiled=True),
    )
    return (
        output,
        input_grad,
        reduced[0],
        reduced[1],
        reduced[2],
        reduced[3],
        experts_grad,
        reduced[4],
        reduced[5],
    )


def solution(mesh):
    placed = (
        P(("shard", "tensor"), None, None),
        P(None, ("shard", "tensor")),
        P(None, ("shard", "tensor")),
        P(None, ("shard", "tensor"), "heads"),
        P(("shard", "tensor"), "heads"),
        P("shard", None, "heads", "tensor"),
        P("heads", ("shard", "tensor")),
        P("heads", ("shard", "tensor")),
        P(("shard", "tensor"), None, None),
    )
    return jax.shard_map(
        shards,
        mesh=mesh,
        in_specs=placed,
        out_specs=(
            P(("shard", "tensor"), None, None),
            P(("shard", "tensor"), None, None),
            P(None, ("shard", "tensor")),
            P(None, ("shard", "tensor")),
            P(None, ("shard", "tensor"), "heads"),
            P(("shard", "tensor"), "heads"),
            P("shard", None, "heads", "tensor"),
            P("heads", ("shard", "tensor")),
            P("heads", ("shard", "tensor")),
        ),
        check_vma=False,
    )
```

profile of v0, /device:TPU:0, one launch (start us, length us, event | category | flops | bytes accessed | tf_op | source)
XLA Modules:
  0.0 2830.2 jit_solution(6276251070341257585)
XLA Ops:
  7.2 1.9 copy.269
  9.2 13.2 all-gather.2
  22.5 11.0 all-gather.3
  34.2 2.4 convert_reduce_fusion
  38.9 2.3 slice.54
  41.7 3.5 copy.332
  45.2 4.2 convert_bitcast_fusion
  55.2 3.1 fusion.93
  58.4 178.4 %all-reduce.5.cloned.1.call-done = f32[8,197,768]{2,1,0:T(8,128)} async-done(((f32[8,197,768]{2,1,0:T(8,128)}), f32[8,197,768]{2,1,0:T(8,128)}) %all-reduce.5.cloned.1.call-update) | async-done | bytes 4841488 | tf_op jit(solution)/shard_map/psum | solution.py:99
  236.8 3.5 fusion.106
  241.0 1.5 copy-done
  243.6 1.5 copy-done.8
  245.0 1.9 copy.273
  247.3 20.9 copy.281
  269.0 13.9 all-gather.4
  283.0 15.7 all_gather.50
  299.3 11.4 all-gather.12.cloned.1.call-done
  310.7 3.8 fusion.108
  316.7 6.3 fusion.67
  323.0 431.2 %all-gather.14.cloned.1.call-done = bf16[768,2,16,1536]{3,0,2,1:T(8,128)(2,1)} async-done(((bf16[192,2,16,1536]{3,0,2,1:T(8,128)(2,1)}), bf16[768,2,16,1536]{3,0,2,1:T(8,128)(2,1)}) %all-gather.14.cloned.1.call-update) | async-done | bytes 75497488 | tf_op jit(solution)/shard_map/all_gather | solution.py:45
  754.3 13.9 fusion.27
  768.2 16.9 fusion.66
  785.2 13.1 all-gather.5
  799.3 13.2 all-gather.1
  812.5 13.1 all-gather
  827.1 2.5 fusion.35
  831.7 3.1 convert_reduce_fusion.2
  834.9 6.5 all_gather.52
  841.4 16.6 convert_reduce_fusion.1
  857.9 16.3 fusion.73
  875.0 4.6 fusion.21
  879.6 2.0 copy.297
  882.8 1.6 subtract_multiply_fusion.1
  885.4 5.3 fusion.86
  891.6 21.6 psum.37
  913.3 2.1 fusion.82
  915.7 113.1 %reduce-scatter.23.cloned.1.call-done = f32[8,197,768]{2,1,0:T(8,128)} async-done(((f32[16,197,768]{2,1,0:T(8,128)}), f32[8,197,768]{2,1,0:T(8,128)}) %reduce-scatter.23.cloned.1.call-update) | async-done | bytes 4841488 | tf_op jit(solution)/shard_map/reduce_scatter | solution.py:168
  1028.8 5.5 convolution_add_fusion
  1035.2 3.1 fusion.96
  1038.3 174.4 %all-reduce.7.cloned.1.call-done = f32[8,197,768]{2,1,0:T(8,128)} async-done(((f32[8,197,768]{2,1,0:T(8,128)}), f32[8,197,768]{2,1,0:T(8,128)}) %all-reduce.7.cloned.1.call-update) | async-done | bytes 4841488 | tf_op jit(solution)/shard_map/psum | solution.py:178
  1212.8 5.1 multiply_reduce_fusion
  1218.8 3.9 multiply_add_fusion
  1231.2 4.5 convolution_bitcast_fusion.2
  1237.5 1.9 convolution_bitcast_fusion.5
  1239.7 4.1 convolution_bitcast_fusion.4
  1244.0 2.7 convolution_bitcast_fusion.3
  1246.8 1.6 pad_maximum_fusion.2
  1248.3 4.5 copy.325
  1252.8 4.7 reshape.134
  1258.6 28.4 %convolution_bitcast_fusion.1 = f32[768,1,16,1536]{0,3,2,1:T(8,128)} fusion(bf16[16,16,1536]{2,0,1:T(8,128)(2,1)} %copy-done.18, bf16[16,16,768]{2,1,0:T(8,128)(2,1)S(1)} %copy-done.17), kind=kOutput, calls=%fused_computation.9 | convolution fusion | flops 603979776 | bytes 76677120 | tf_op jit(solution)/shard_map/ned,nef->def/dot_general | solution.py:151
  1287.0 30.6 %convolution_bitcast_fusion = f32[768,1,16,1536]{0,3,2,1:T(8,128)} fusion(bf16[16,16,768]{2,1,0:T(8,128)(2,1)S(1)} %copy-done.26, f32[16,16,1536]{2,1,0:T(8,128)} %copy-done.16), kind=kOutput, calls=%fused_computation.8 | convolution fusion | flops 629538816 | bytes 77463552 | tf_op jit(solution)/shard_map/ned,nef->def/dot_general | solution.py:152
  1317.6 255.2 %all-reduce.9.cloned.1.call-done = (f32[8,197,768]{2,1,0:T(8,128)}, f32[8,197,768]{2,1,0:T(8,128)}) async-done(((f32[8,197,768]{2,1,0:T(8,128)}, f32[8,197,768]{2,1,0:T(8,128)}), (f32[8,197,768]{2,1,0:T(8,128)}, f32[8,197,768]{2,1,0:T(8,128)})) %all-reduce.9.cloned.1.call-update) | async-done | bytes 9682960 | tf_op jit(solution)/shard_map/psum | solution.py:129
  1572.9 5.1 fusion.19
  1581.1 100.0 %pad_maximum_fusion = f32[768,2,16,1536]{0,3,2,1:T(8,128)} fusion(f32[768,1,16,1536]{0,3,2,1:T(8,128)} %convolution_bitcast_fusion, f32[768,1,16,1536]{0,3,2,1:T(8,128)} %convolution_bitcast_fusion.1), kind=kLoop, calls=%fused_computation.5 | loop fusion | flops 37748736 | bytes 301989888 | tf_op jit(solution)/shard_map/stack | solution.py:156
  1681.1 149.8 %copy.311 = f32[768,2,16,1536]{3,2,1,0:T(8,128)} copy(f32[768,2,16,1536]{0,3,2,1:T(8,128)} %pad_maximum_fusion) | data formatting | bytes 301989888 | tf_op jit(solution)/shard_map/stack | solution.py:156
  1830.9 1.5 copy.330
  1832.4 1.5 copy.328
  1836.0 6.8 add_convert_fusion
  1842.9 1.9 copy.312
  1845.9 1.5 slice-done.4
  1848.0 1.5 copy-done.5
  1849.6 2.0 fusion.18
  1851.6 1.9 copy.313
  1856.4 967.1 %reduce-scatter.27.cloned.1.call-done = f32[192,2,16,1536]{3,2,1,0:T(8,128)} async-done(((f32[768,2,16,1536]{3,2,1,0:T(8,128)}), f32[192,2,16,1536]{3,2,1,0:T(8,128)}) %reduce-scatter.27.cloned.1.call-update) | async-done | bytes 37748752 | tf_op jit(solution)/shard_map/reduce_scatter | solution.py:155
  (283 shorter events, 47.1 us)
Async XLA Ops:
  7.2 29.5 %copy-start.3 = (bf16[8,197,768]{2,0,1:T(8,128)(2,1)S(1)}, bf16[8,197,768]{2,0,1:T(8,128)(2,1)}, u32[]{:S(2)}) copy-start(bf16[8,197,768]{2,0,1:T(8,128)(2,1)} %param.11) | copy-start | bytes 7262212
  7.2 31.7 %all-gather.10.cloned.1.call-start = ((), (), s32[]{:S(2)}) async-start(), calls=%async_computation.10 | async-start | bytes 1769472 | tf_op jit(solution)/shard_map/all_gather | solution.py:64
  9.2 227.6 %all-reduce.5.cloned.1.call-start = ((), (), s32[]{:S(2)}) async-start(), calls=%async_computation.11 | async-start | bytes 9830400 | tf_op jit(solution)/shard_map/psum | solution.py:99
  34.2 10.9 copy-start.70
  34.2 10.9 copy-start.79
  34.2 206.8 %copy-start.68 = (f32[768]{0:T(1024)}, f32[768]{0:T(1024)S(1)}, u32[]{:S(2)}) copy-start(f32[768]{0:T(1024)S(1)} %get-tuple-element.261) | copy-start | bytes 9220
  36.7 8.4 copy-start.55
  37.7 7.4 copy-start.65
  58.3 252.4 %all-gather.12.cloned.1.call-start = ((), (), s32[]{:S(2)}) async-start(), calls=%async_computation.12 | async-start | bytes 7262208 | tf_op jit(solution)/shard_map/all_gather | solution.py:103
  246.9 507.3 %all-gather.14.cloned.1.call-start = ((), (), s32[]{:S(2)}) async-start(), calls=%async_computation.13 | async-start | bytes 94371840 | tf_op jit(solution)/shard_map/all_gather | solution.py:45
  268.3 14.7 copy-start.76
  268.3 557.7 %reduce-scatter.21.cloned.1.call-start = ((), (), s32[]{:S(2)}) async-start(), calls=%async_computation.14 | async-start | bytes 1179648 | tf_op jit(solution)/shard_map/reduce_scatter | solution.py:118
  283.0 31.5 %copy-start.48 = (bf16[768,16,1]{0,1,2:T(8,128)(2,1)}, bf16[768,16,1]{0,1,2:T(8,128)(2,1)S(1)}, u32[]{:S(2)}) copy-start(bf16[768,16,1]{0,1,2:T(8,128)(2,1)S(1)} %reshape.124) | copy-start | bytes 73732
  316.7 6.3 copy-start.27
  768.1 17.0 copy-start.16
  768.2 17.0 copy-start.78
  785.1 128.1 %reduce-scatter.25.cloned.1.call-start = ((), (), s32[]{:S(2)}) async-start(), calls=%async_computation.16 | async-start | bytes 2420736 | tf_op jit(solution)/shard_map/reduce_scatter | solution.py:169
  825.9 4.2 copy-start.29
  826.0 4.0 copy-start.31
  830.0 4.8 copy-start.10
  831.7 9.7 copy-start.43
  841.4 16.6 copy-start.25
  857.9 16.3 copy-start.18
  884.4 144.4 %reduce-scatter.23.cloned.1.call-start = ((), (), s32[]{:S(2)}) async-start(), calls=%async_computation.15 | async-start | bytes 14745600 | tf_op jit(solution)/shard_map/reduce_scatter | solution.py:168
  890.7 22.5 copy-start.11
  890.7 22.5 copy-start.30
  890.7 22.5 copy-start.32
  890.8 322.0 %all-reduce.7.cloned.1.call-start = ((), (), s32[]{:S(2)}) async-start(), calls=%async_computation.17 | async-start | bytes 9830400 | tf_op jit(solution)/shard_map/psum | solution.py:178
  913.2 115.6 %copy-start.49 = (bf16[768,16,1]{0,1,2:T(8,128)(2,1)S(1)}, bf16[768,16,1]{0,1,2:T(8,128)(2,1)}, u32[]{:S(2)}) copy-start(bf16[768,16,1]{0,1,2:T(8,128)(2,1)} %copy-done.48) | copy-start | bytes 73732
  915.7 118.6 %copy-start.46 = (bf16[8,197,16]{1,2,0:T(8,128)(2,1)}, bf16[8,197,16]{1,2,0:T(8,128)(2,1)S(1)}, u32[]{:S(2)}) copy-start(bf16[8,197,16]{1,2,0:T(8,128)(2,1)S(1)} %copy.301) | copy-start | bytes 151300
  1034.3 538.6 %all-reduce.9.cloned.1.call-start = ((), (), s32[]{:S(2)}) async-start(), calls=%async_computation.25 | async-start | bytes 19660800 | tf_op jit(solution)/shard_map/psum | solution.py:129
  1035.2 177.5 %copy-start.53 = (f32[8,197]{1,0:T(8,128)S(1)}, f32[8,197]{1,0:T(8,128)}, u32[]{:S(2)}) copy-start(f32[8,197]{1,0:T(8,128)} %copy-done.52) | copy-start | bytes 18916
  1035.2 177.5 %copy-start.63 = (f32[8,197]{1,0:T(8,128)S(1)}, f32[8,197]{1,0:T(8,128)}, u32[]{:S(2)}) copy-start(f32[8,197]{1,0:T(8,128)} %copy-done.62) | copy-start | bytes 18916
  1035.2 177.5 %copy-start.69 = (f32[768]{0:T(1024)S(1)}, f32[768]{0:T(1024)}, u32[]{:S(2)}) copy-start(f32[768]{0:T(1024)} %copy-done.68) | copy-start | bytes 9220
  1212.7 5.3 copy-start.6
  1212.8 6.0 copy-start.7
  1217.9 7.0 slice-start
  1218.8 6.1 slice-start.1
  1226.0 4.3 copy-start.36
  1235.7 595.3 %reduce-scatter.39.cloned.1.call-start = ((), (), s32[]{:S(2)}) async-start(), calls=%async_computation.24 | async-start | bytes 442368
  1237.4 595.0 %reduce-scatter.37.cloned.1.call-start = ((), (), s32[]{:S(2)}) async-start(), calls=%async_computation.23 | async-start | bytes 442368
  1239.4 4.5 copy-start.4
  1239.4 4.5 copy-start.56
  1239.4 4.5 copy-start.66
  1239.4 4.5 copy-start.71
  1239.4 4.5 copy-start.80
  1239.4 594.5 %reduce-scatter.35.cloned.1.call-start = ((), (), s32[]{:S(2)}) async-start(), calls=%async_computation.22 | async-start | bytes 2654208
  1239.6 4.2 copy-start.37
  1239.6 4.2 copy-start.40
  1239.7 4.4 copy-start.42
  1257.6 29.4 %copy-start.26 = (bf16[16,16,768]{2,1,0:T(8,128)(2,1)S(1)}, bf16[16,16,768]{2,1,0:T(8,128)(2,1)}, u32[]{:S(2)}) copy-start(bf16[16,16,768]{2,1,0:T(8,128)(2,1)} %copy-done.25) | copy-start | bytes 1179652
  1257.6 595.9 %reduce-scatter.33.cloned.1.call-start = ((), (), s32[]{:S(2)}) async-start(), calls=%async_computation.21 | async-start | bytes 442368
  1579.0 275.9 %reduce-scatter.31.cloned.1.call-start = ((), (), s32[]{:S(2)}) async-start(), calls=%async_computation.20 | async-start | bytes 442368
  1580.1 276.3 %reduce-scatter.29.cloned.1.call-start = ((), (), s32[]{:S(2)}) async-start(), calls=%async_computation.19 | async-start | bytes 221184 | tf_op jit(solution)/shard_map/reduce_scatter | solution.py:250
  1580.9 1242.6 %reduce-scatter.27.cloned.1.call-start = ((), (), s32[]{:S(2)}) async-start(), calls=%async_computation.18 | async-start | bytes 188743680 | tf_op jit(solution)/shard_map/reduce_scatter | solution.py:155
  1836.0 9.9 slice-start.2
  1836.0 11.4 slice-start.4
  1836.0 11.7 slice-start.3
  1836.0 12.0 slice-start.5
  1842.9 3.0 copy-start.73
  1842.9 6.7 copy-start.5
  1842.9 6.7 copy-start.57
  1842.9 6.7 copy-start.67
  1842.9 6.7 copy-start.72
  (39 other events, 55.9 us)
Sparse Core Ops, SparseCore 0:
  10.5 28.3 all-gather.9
  58.4 178.2 all-reduce.4
  247.1 63.6 all-gather.11
  312.8 441.3 all-gather.13
  785.3 17.4 reduce-scatter.20
  884.5 26.3 reduce-scatter.24
  913.9 114.7 reduce-scatter.22
  1034.4 178.2 all-reduce.6
  1235.8 337.0 all-reduce.8
  1575.8 32.8 reduce-scatter.38
  1611.7 33.7 reduce-scatter.36
  1649.3 42.4 reduce-scatter.34
  1695.2 33.8 reduce-scatter.32
  1732.3 33.8 reduce-scatter.30
  1769.9 32.6 reduce-scatter.28
  1831.0 992.3 reduce-scatter.26
where the time goes:
time: 2840 us; the launch traced here: 2830 us
  waiting for transfers between devices  2130 us (75%)
  local copies, waits for them, and re-layouts  230 us (8%)
  matrix products  184 us (6%)
  other arithmetic  145 us (5%)
  blocking collectives  121 us (4%)
    reduce_scatter x1, waiting for transfers between devices, shards(): lax.psum_scatter(jnp.stack((input_term, output_term), axis=1), 'shard', s...  967 us
    all_gather x1, waiting for transfers between devices, fetch_experts(): return lax.all_gather(experts, 'shard', axis=0, tiled=True)  431 us
    psum x1, waiting for transfers between devices, shards(): mixed = lax.psum(mixed_part, 'heads')  255 us
    psum x1, waiting for transfers between devices, shards(): attended = lax.psum(attn_part, 'heads')  178 us
    psum x1, waiting for transfers between devices, shards(): grad_normed_two = lax.psum(grad_tokens, 'heads')  174 us
    another operation x1, local copies, waits for them, and re-layouts, shards(): jnp.stack((input_term, output_term), axis=1)  150 us
    reduce_scatter x1, waiting for transfers between devices, shards(): lax.psum_scatter(grad_tokens_pair, 'tensor', scatter_dimension=0, tiled=T...  113 us
    another operation x1, other arithmetic, shards(): jnp.stack((input_term, output_term), axis=1)  100 us
  transfers between devices with their start and end apart: 16, of which 8 were waited for; matrix products, arithmetic and copies ran while one was open for 14% of the time, Pallas kernels for 0%

commit v1 on v0

v1 whole, which is shorter than its diff:
```python
from functools import partial

import jax
import jax.numpy as jnp
from jax import lax
from jax.sharding import PartitionSpec as P

HEAD_DIM = 64
F32 = jnp.float32
BF16 = jnp.bfloat16
ROWS = ("shard", "tensor")
epsilon = 1e-06
einsum = partial(jnp.einsum, preferred_element_type=F32)


def normalize(values, scale, shift):
    centered = values - jnp.mean(values, axis=-1, keepdims=True)
    variance = jnp.mean(centered * centered, axis=-1, keepdims=True)
    inverse = lax.rsqrt(variance + epsilon)
    unit_part = centered * inverse
    return (unit_part * scale + shift, unit_part, inverse)


def normalize_back(grad_output, unit_part, inverse, scale):
    scaled = grad_output * scale
    average = jnp.mean(scaled, axis=-1, keepdims=True)
    projection = jnp.mean(scaled * unit_part, axis=-1, keepdims=True)
    grad_input = inverse * (scaled - average - unit_part * projection)
    return (
        grad_input,
        jnp.sum(grad_output * unit_part, axis=(0, 1)),
        jnp.sum(grad_output, axis=(0, 1)),
    )


def to_experts(slots):
    slots = lax.all_to_all(slots, "heads", split_axis=1, concat_axis=0, tiled=True)
    slots = lax.all_to_all(slots, "shard", split_axis=2, concat_axis=0, tiled=True)
    return lax.all_gather(slots, "tensor", axis=0, tiled=True)


def to_images(slots):
    slots = lax.psum_scatter(slots, "tensor", scatter_dimension=0, tiled=True)
    slots = lax.all_to_all(slots, "shard", split_axis=0, concat_axis=2, tiled=True)
    return lax.all_to_all(slots, "heads", split_axis=0, concat_axis=1, tiled=True)


def shards(tokens, norm_scales, norm_biases, w_attn, phi, experts, in_bias, out_bias, cotangent):
    heads_n = lax.axis_size("heads")
    group, seq_len, width = tokens.shape
    own = group // heads_n
    heads_index = lax.axis_index("heads")
    tensor_index = lax.axis_index("tensor")
    shard_index = lax.axis_index("shard")
    hidden = experts.shape[3]
    rows = experts.shape[0]
    scales, biases, in_full = (
        lax.all_gather(norm_scales, ROWS, axis=1, tiled=True).astype(F32),
        lax.all_gather(norm_biases, ROWS, axis=1, tiled=True).astype(F32),
        lax.all_gather(in_bias, ROWS, axis=1, tiled=True).astype(F32),
    )
    attn = lax.all_gather(
        lax.all_gather(w_attn, "heads", axis=2, tiled=True), ROWS, axis=1, tiled=True
    )
    phi_full = lax.all_gather(
        lax.all_gather(phi, "heads", axis=1, tiled=True), ROWS, axis=0, tiled=True
    )
    out_rows = lax.all_gather(out_bias, "tensor", axis=1, tiled=True).astype(F32)
    e_own = experts.shape[2] // lax.axis_size("shard") if experts.shape[2] % lax.axis_size("shard") == 0 else 0
    in_local = lax.dynamic_slice_in_dim(in_full, tensor_index * hidden, hidden, 1)
    factor = HEAD_DIM ** (-0.5)
    tokens = lax.dynamic_slice_in_dim(tokens, heads_index * own, own, 0)
    cotangent = lax.dynamic_slice_in_dim(cotangent, heads_index * own, own, 0)
    n_heads = width // HEAD_DIM
    inputs = tokens.astype(F32)
    normed_one, unit_one, inverse_one = normalize(inputs, scales[0], biases[0])
    normed_one_b = normed_one.astype(BF16)
    projected = einsum("nsd,kdc->knsc", normed_one_b, attn[:3]).astype(BF16)
    query, keyed, valued = projected.reshape(3, own, seq_len, n_heads, HEAD_DIM)
    scores = einsum("nqhe,nkhe->nhqk", query, keyed) * factor
    score_peak = jnp.max(scores, axis=-1, keepdims=True)
    exponent = jnp.exp(scores - score_peak)
    probs = exponent / jnp.sum(exponent, axis=-1, keepdims=True)
    probs_b = probs.astype(BF16)
    context_b = (
        einsum("nhqk,nkhe->nqhe", probs_b, valued).astype(BF16).reshape(own, seq_len, width)
    )
    hidden_one = inputs + einsum("nsc,dc->nsd", context_b, attn[3])
    normed_two, unit_two, inverse_two = normalize(hidden_one, scales[1], biases[1])
    normed_two_b = normed_two.astype(BF16)
    logits = einsum("nsd,de->nse", normed_two_b, phi_full)
    dispatch = jax.nn.softmax(logits, axis=1)
    dispatch_b = dispatch.astype(BF16)
    combine = jax.nn.softmax(logits, axis=2)
    combine_b = combine.astype(BF16)
    slot_in = to_experts(einsum("nse,nsd->ned", dispatch_b, normed_two_b).astype(BF16))
    share = 1 if e_own else 0

    def meet(partial_sum):
        return lax.psum_scatter(partial_sum, "shard", scatter_dimension=share, tiled=True)

    def spread(values):
        return lax.all_gather(values, "shard", axis=share, tiled=True)

    pre = meet(einsum("ned,def->nef", slot_in, experts[:, 0]))
    if e_own:
        pre = pre + lax.dynamic_slice_in_dim(in_local, shard_index * e_own, e_own, 0)
    else:
        pre = pre + in_local
    gelu_value, gelu_back = jax.vjp(partial(jax.nn.gelu, approximate=False), pre)
    activated = spread(gelu_value.astype(BF16))
    slot_out_part = einsum("nef,def->ned", activated, experts[:, 1])
    slot_out_part = slot_out_part + jnp.where(tensor_index == 0, out_rows, 0.0)
    slot_out = to_images(slot_out_part).astype(BF16)
    output = (hidden_one + einsum("nse,ned->nsd", combine_b, slot_out)).astype(BF16)
    output = lax.all_gather(output, "heads", axis=0, tiled=True)
    grad_combine = einsum("nsd,ned->nse", cotangent, slot_out)
    grad_slot = to_experts(einsum("nse,nsd->ned", combine_b, cotangent).astype(BF16))
    grad_act = meet(einsum("ned,def->nef", grad_slot, experts[:, 1]))
    grad_pre = spread(gelu_back(grad_act)[0].astype(BF16))
    grad_slot_in = einsum("nef,def->ned", grad_pre, experts[:, 0]).astype(BF16)
    input_term = einsum("ned,nef->def", slot_in, grad_pre)
    output_term = einsum("ned,nef->def", grad_slot, activated)
    experts_grad = jnp.stack((input_term, output_term), axis=1)
    grad_slot_in = to_images(grad_slot_in.astype(F32)).astype(BF16)
    in_bias_grad = lax.dynamic_slice_in_dim(
        lax.all_gather(jnp.sum(grad_pre.astype(F32), axis=0), "tensor", axis=1, tiled=True),
        (shard_index * lax.axis_size("tensor") + tensor_index) * in_bias.shape[1],
        in_bias.shape[1],
        1,
    )
    out_bias_grad = lax.dynamic_slice_in_dim(
        jnp.sum(grad_slot.astype(F32), axis=0),
        tensor_index * out_bias.shape[1],
        out_bias.shape[1],
        1,
    )
    grad_dispatch = einsum("nsd,ned->nse", normed_two_b, grad_slot_in)
    grad_logits = (
        dispatch * (grad_dispatch - jnp.sum(dispatch * grad_dispatch, axis=1, keepdims=True))
        + combine * (grad_combine - jnp.sum(combine * grad_combine, axis=2, keepdims=True))
    ).astype(BF16)
    phi_grad = einsum("nsd,nse->de", normed_two_b, grad_logits)
    grad_normed_two = einsum("nse,ned->nsd", dispatch_b, grad_slot_in) + einsum(
        "nse,de->nsd", grad_logits, phi_full
    )
    grad_hidden_norm, scale_two_grad, bias_two_grad = normalize_back(
        grad_normed_two, unit_two, inverse_two, scales[1]
    )
    grad_hidden = cotangent.astype(F32) + grad_hidden_norm
    grad_hidden_b = grad_hidden.astype(BF16)
    out_weight_grad = einsum("nsd,nsc->dc", grad_hidden_b, context_b)
    grad_context = einsum("nsd,dc->nsc", grad_hidden_b, attn[3]).astype(BF16)
    grad_context = grad_context.reshape(own, seq_len, n_heads, HEAD_DIM)
    grad_value = einsum("nhqk,nqhe->nkhe", probs_b, grad_context).astype(BF16)
    grad_probs = einsum("nqhe,nkhe->nhqk", grad_context, valued)
    grad_scores = (
        probs * (grad_probs - jnp.sum(probs * grad_probs, axis=-1, keepdims=True))
    ).astype(BF16)
    grad_query = (einsum("nhqk,nkhe->nqhe", grad_scores, keyed) * factor).astype(BF16)
    grad_key = (einsum("nhqk,nqhe->nkhe", grad_scores, query) * factor).astype(BF16)
    grad_proj = jnp.stack((grad_query, grad_key, grad_value)).reshape(3, own, seq_len, width)
    proj_grad = einsum("nsd,knsc->kdc", normed_one_b, grad_proj)
    grad_normed_one = einsum("knsc,kdc->nsd", grad_proj, attn[:3])
    grad_input_norm, scale_one_grad, bias_one_grad = normalize_back(
        grad_normed_one, unit_one, inverse_one, scales[0]
    )
    input_grad = (grad_hidden + grad_input_norm).astype(BF16)
    input_grad = lax.all_gather(input_grad, "heads", axis=0, tiled=True)
    attn_grad = jnp.concatenate((proj_grad, out_weight_grad[None]), axis=0)
    attn_grad = lax.psum_scatter(attn_grad, ROWS, scatter_dimension=1, tiled=True)
    attn_grad = lax.psum_scatter(attn_grad, "heads", scatter_dimension=2, tiled=True)
    phi_grad = lax.psum_scatter(phi_grad, ROWS, scatter_dimension=0, tiled=True)
    phi_grad = lax.psum_scatter(phi_grad, "heads", scatter_dimension=1, tiled=True)
    norms = jnp.stack((scale_one_grad, scale_two_grad, bias_one_grad, bias_two_grad))
    norms = lax.psum(lax.psum_scatter(norms, ROWS, scatter_dimension=1, tiled=True), "heads")
    return (
        output,
        input_grad,
        norms[:2],
        norms[2:],
        attn_grad,
        phi_grad,
        experts_grad,
        in_bias_grad,
        out_bias_grad,
    )


def solution(mesh):
    images = P(ROWS, None, None)
    return jax.shard_map(
        shards,
        mesh=mesh,
        in_specs=(
            images,
            P(None, ROWS),
            P(None, ROWS),
            P(None, ROWS, "heads"),
            P(ROWS, "heads"),
            P("shard", None, "heads", "tensor"),
            P("heads", ROWS),
            P("heads", ROWS),
            images,
        ),
        out_specs=(
            images,
            images,
            P(None, ROWS),
            P(None, ROWS),
            P(None, ROWS, "heads"),
            P(ROWS, "heads"),
            P("shard", None, "heads", "tensor"),
            P("heads", ROWS),
            P("heads", ROWS),
        ),
        check_vma=False,
    )
```

time: 2840 us -> 889 us (0.31)
  waiting for transfers between devices: 2130 us -> 283 us
  other arithmetic: 145 us -> 39.2 us
  blocking collectives: 121 us -> 171 us
  matrix products: 184 us -> 135 us
    reduce_scatter x5, waiting for transfers between devices: 1080 us -> 71.9 us  [the longest x2 41 us: meet(): lax.psum_scatter(partial_sum, 'shard', scatter_dimension=share, tiled=True)]
    psum x3 -> x0, waiting for transfers between devices: 608 us -> none  [the longest x1 255 us: shards(): mixed = lax.psum(mixed_part, 'heads')]
    all_gather x3 -> x5, waiting for transfers between devices: 444 us -> 61.4 us  [the longest x2 42.7 us: spread(): return lax.all_gather(values, 'shard', axis=share, tiled=True)]
    another operation x6 -> x11, local copies, waits for them, and re-layouts: 150 us -> 10.7 us  [the longest x3 6.69 us: shards(): jnp.stack((grad_query, grad_key, grad_value))]
    unnamed x21 -> x18, waiting for transfers between devices: 0.29 us -> 134 us
    another operation x3 -> x2, other arithmetic: 100 us -> 15.3 us  [the longest x1 15.2 us: shards(): experts_grad = jnp.stack((input_term, output_term), axis=1)]
    unnamed x192 -> x96, local copies, waits for them, and re-layouts: 71.4 us -> 151 us
    dot_general x27 -> x25, matrix products: 184 us -> 128 us  [the longest x1 17 us: shards(): pre = meet(einsum('ned,def->nef', slot_in, experts[:, 0]))]
  transfers between devices with their start and end apart: 16 -> 19, of which waited for: 8 -> 12; matrix products, arithmetic and copies ran while one was open for 14% -> 31% of each run, Pallas kernels for 0% -> 0%
where the time goes in v1:
time: 889 us; the launch traced here: 877 us
  waiting for transfers between devices  283 us (32%)
  local copies, waits for them, and re-layouts  214 us (24%)
  blocking collectives  171 us (19%)
  matrix products  135 us (15%)
  other arithmetic  39.2 us (4%)
  starting transfers between devices  19.8 us (2%)
  between operations  15.8 us (2%)
    unnamed x96, local copies, waits for them, and re-layouts  151 us
    unnamed x18, waiting for transfers between devices  134 us
    all_gather x2, waiting for transfers between devices, spread(): return lax.all_gather(values, 'shard', axis=share, tiled=True)  42.7 us
    reduce_scatter x2, waiting for transfers between devices, meet(): lax.psum_scatter(partial_sum, 'shard', scatter_dimension=share, tiled=True)  41 us
    all_to_all x2, blocking collectives, to_experts(): lax.all_to_all(slots, 'heads', split_axis=1, concat_axis=0, tiled=True)  31.5 us
    reduce_scatter x2, waiting for transfers between devices, to_images(): slots = lax.psum_scatter(slots, 'tensor', scatter_dimension=0, tiled=True)  29.8 us
    all_gather x1, blocking collectives, shards(): lax.all_gather(w_attn, 'heads', axis=2, tiled=True)  21.4 us
    all_gather x1, waiting for transfers between devices, shards(): input_grad = lax.all_gather(input_grad, 'heads', axis=0, tiled=True)  18.7 us
  transfers between devices with their start and end apart: 19, of which 12 were waited for; matrix products, arithmetic and copies ran while one was open for 31% of the time, Pallas kernels for 0%

profile of v1, /device:TPU:0, one launch (start us, length us, event | category | flops | bytes accessed | tf_op | source)
XLA Modules:
  0.0 877.4 jit_solution(12841294151314626580)
XLA Ops:
  8.5 21.4 %all_gather.47 = bf16[4,96,768]{1,0,2:T(4,128)(2,1)S(1)} all-gather(bf16[4,96,192]{1,0,2:T(4,128)(2,1)S(1)} %copy.221), channel_id=1, replica_groups=mesh['shard'=4,'heads'=4,'tensor'=2] {'heads'}, dimensions={2}, use_global_device_ids=true | all-gather | bytes 737280 | tf_op jit(solution)/shard_map/all_gather | solution.py:63
  31.2 11.8 %all-gather = bf16[8,96,2]{1,2,0:T(2,128)(2,1)S(1)} all-gather(bf16[1,96,2]{1,2,0:T(2,128)(2,1)S(1)} %bitcast.244), channel_id=1, replica_groups=mesh['shard'=4,'heads'=4,'tensor'=2] {'shard','tensor'}, dimensions={0}, use_global_device_ids=true | all-gather | bytes 3456 | tf_op jit(solution)/shard_map/all_gather | solution.py:58
  43.1 11.5 %all-gather.1 = bf16[8,96,2]{1,2,0:T(2,128)(2,1)S(1)} all-gather(bf16[1,96,2]{1,2,0:T(2,128)(2,1)S(1)} %bitcast.245), channel_id=1, replica_groups=mesh['shard'=4,'heads'=4,'tensor'=2] {'shard','tensor'}, dimensions={0}, use_global_device_ids=true | all-gather | bytes 3456 | tf_op jit(solution)/shard_map/all_gather | solution.py:59
  54.7 13.1 %all_gather.49 = bf16[96,64]{0,1:T(8,128)(2,1)S(1)} all-gather(bf16[96,16]{0,1:T(8,128)(2,1)S(1)} %copy-done.28), channel_id=1, replica_groups=mesh['shard'=4,'heads'=4,'tensor'=2] {'heads'}, dimensions={1}, use_global_device_ids=true | all-gather | bytes 15360 | tf_op jit(solution)/shard_map/all_gather | solution.py:66
  67.8 16.0 %all-gather.2 = bf16[8,96,64]{1,2,0:T(8,128)(2,1)S(1)} all-gather(bf16[1,96,64]{1,2,0:T(8,128)(2,1)S(1)} %bitcast.238), channel_id=1, replica_groups=mesh['shard'=4,'heads'=4,'tensor'=2] {'shard','tensor'}, dimensions={0}, use_global_device_ids=true | all-gather | bytes 110592 | tf_op jit(solution)/shard_map/all_gather | solution.py:65
  85.3 3.8 convert_bitcast_fusion
  93.2 4.1 fusion.86
  97.3 3.0 convolution_convert_fusion.1
  100.3 2.5 fusion.87
  105.6 11.0 %all_to_all.126 = bf16[2,64,768]{2,0,1:T(2,128)(2,1)S(1)} all-to-all(bf16[2,64,768]{2,0,1:T(2,128)(2,1)S(1)} %copy.229), channel_id=1, replica_groups=mesh['shard'=4,'heads'=4,'tensor'=2] {'heads'}, dimensions={1} | all-to-all | bytes 393216 | tf_op jit(solution)/shard_map/all_to_all | solution.py:37
  120.0 3.4 all-to-all-start.1
  123.4 14.6 %fusion.83 = (bf16[192,1,16,1536]{3,2,1,0:T(8,128)(2,1)}, bf16[192,1,16,1536]{3,2,1,0:T(8,128)(2,1)}) fusion(bf16[192,2,16,1536]{3,2,1,0:T(8,128)(2,1)} %param.14), kind=kLoop, calls=%fused_computation.156 | loop fusion | bytes 37748736 | tf_op jit(solution)/shard_map/slice | solution.py:105
  141.0 9.6 %all_gather.51 = bf16[64,16,192]{2,0,1:T(8,128)(2,1)S(1)} all-gather(bf16[32,16,192]{2,0,1:T(8,128)(2,1)S(1)} %bitcast.214), channel_id=1, replica_groups=mesh['shard'=4,'heads'=4,'tensor'=2] {'tensor'}, dimensions={0}, use_global_device_ids=true | all-gather | bytes 589824 | tf_op jit(solution)/shard_map/all_gather | solution.py:39
  150.6 17.0 %fusion.11 = f32[64,16,1536]{2,0,1:T(8,128)} fusion(bf16[64,16,192]{2,0,1:T(8,128)(2,1)S(1)} %all_gather.51, bf16[192,1,16,1536]{3,2,1,0:T(8,128)(2,1)} %get-tuple-element.77), kind=kOutput, calls=%fused_computation.22 | convolution fusion | flops 603979776 | bytes 16121856 | tf_op jit(solution)/shard_map/ned,def->nef/dot_general | solution.py:105
  167.6 2.3 constant_dynamic-slice_fusion.2
  171.2 20.5 %all_to_all.127 = bf16[2,64,768]{2,0,1:T(2,128)(2,1)S(1)} all-to-all(bf16[2,64,768]{2,0,1:T(2,128)(2,1)S(1)} %copy.242), channel_id=1, replica_groups=mesh['shard'=4,'heads'=4,'tensor'=2] {'heads'}, dimensions={1} | all-to-all | bytes 393216 | tf_op jit(solution)/shard_map/all_to_all | solution.py:37
  196.6 11.8 %all_to_all.128 = bf16[4,2,12288]{2,1,0:T(2,128)(2,1)} all-to-all(bf16[4,2,12288]{2,1,0:T(2,128)(2,1)} %reshape.135), channel_id=1, replica_groups=mesh['shard'=4,'heads'=4,'tensor'=2] {'shard'}, dimensions={0} | all-to-all | bytes 393216 | tf_op jit(solution)/shard_map/all_to_all | solution.py:38
  210.7 2.3 copy.275
  214.1 8.5 all_gather.56
  222.6 16.8 %fusion.10 = f32[64,16,1536]{2,0,1:T(8,128)} fusion(bf16[64,16,192]{2,0,1:T(8,128)(2,1)S(1)} %all_gather.56, bf16[192,1,16,1536]{3,2,1,0:T(8,128)(2,1)} %get-tuple-element.78), kind=kOutput, calls=%fused_computation.21 | convolution fusion | flops 603979776 | bytes 16121856 | tf_op jit(solution)/shard_map/ned,def->nef/dot_general | solution.py:119
  240.2 14.1 %all_gather.52 = bf16[16,3072]{1,0:T(8,128)(2,1)S(1)} all-gather(bf16[16,384]{1,0:T(8,128)(2,1)S(1)} %copy-done.24), channel_id=1, replica_groups=mesh['shard'=4,'heads'=4,'tensor'=2] {'shard','tensor'}, dimensions={1}, use_global_device_ids=true | all-gather | bytes 110592 | tf_op jit(solution)/shard_map/all_gather | solution.py:60
  254.4 41.0 %reduce-scatter.19.cloned.1.call-done = f32[64,4,1536]{2,0,1:T(8,128)} async-done(((f32[64,16,1536]{2,0,1:T(8,128)}), f32[64,4,1536]{2,0,1:T(8,128)}) %reduce-scatter.19.cloned.1.call-update) | async-done | bytes 1572880 | tf_op jit(solution)/shard_map/reduce_scatter | solution.py:100
  295.3 6.0 add_convert_fusion
  303.2 4.3 all-gather.3
  307.6 23.6 %all-gather.12.cloned.1.call-done = bf16[64,16,1536]{2,0,1:T(8,128)(2,1)} async-done(((bf16[64,4,1536]{2,0,1:T(8,128)(2,1)}), bf16[64,16,1536]{2,0,1:T(8,128)(2,1)}) %all-gather.12.cloned.1.call-update) | async-done | bytes 3145744 | tf_op jit(solution)/shard_map/all_gather | solution.py:103
  331.2 11.0 %fusion.31 = f32[64,16,192]{2,0,1:T(8,128)} fusion(bf16[64,16,1536]{2,0,1:T(8,128)(2,1)} %all-gather.12.cloned.1.call-done, bf16[192,1,16,1536]{3,2,1,0:T(8,128)(2,1)} %get-tuple-element.78, f32[16,192]{1,0:T(8,128)S(1)} %bitcast.242), kind=kOutput, calls=%fused_computation.66 | convolution fusion | flops 604176384 | bytes 13381632 | tf_op jit(solution)/shard_map/nef,def->ned/dot_general | solution.py:112
  342.7 19.1 %all-gather.16.cloned.1.call-done = bf16[64,16,1536]{2,0,1:T(8,128)(2,1)} async-done(((bf16[64,4,1536]{2,0,1:T(8,128)(2,1)}), bf16[64,16,1536]{2,0,1:T(8,128)(2,1)}) %all-gather.16.cloned.1.call-update) | async-done | bytes 3145744 | tf_op jit(solution)/shard_map/all_gather | solution.py:103
  361.8 11.0 %fusion.35 = f32[64,16,192]{2,0,1:T(8,128)} fusion(bf16[64,16,1536]{2,0,1:T(8,128)(2,1)} %all-gather.16.cloned.1.call-done, bf16[192,1,16,1536]{3,2,1,0:T(8,128)(2,1)} %get-tuple-element.77), kind=kOutput, calls=%fused_computation.71 | convolution fusion | flops 604372992 | bytes 13369344 | tf_op jit(solution)/shard_map/nef,def->ned/dot_general | solution.py:121
  372.8 12.0 %reduce-scatter.17.cloned.1.call-done = f32[32,16,192]{2,0,1:T(8,128)} async-done(((f32[64,16,192]{2,0,1:T(8,128)}), f32[32,16,192]{2,0,1:T(8,128)}) %reduce-scatter.17.cloned.1.call-update) | async-done | bytes 393232 | tf_op jit(solution)/shard_map/reduce_scatter | solution.py:43
  386.9 3.4 all-to-all-start.2
  390.3 17.8 %reduce-scatter.21.cloned.1.call-done = f32[32,16,192]{2,0,1:T(8,128)} async-done(((f32[64,16,192]{2,0,1:T(8,128)}), f32[32,16,192]{2,0,1:T(8,128)}) %reduce-scatter.21.cloned.1.call-update) | async-done | bytes 393232 | tf_op jit(solution)/shard_map/reduce_scatter | solution.py:43
  410.1 3.4 all-to-all-start.6
  414.6 4.9 all-to-all-done.6
  419.5 4.6 all-to-all-start.3
  425.2 6.2 all-to-all-done.3
  431.4 3.4 all-to-all-start.7
  435.7 5.3 all-to-all-done.7
  443.3 2.7 fusion.55
  448.0 3.5 multiply_reduce_fusion.2
  457.1 2.7 convolution_convert_fusion.2
  462.0 4.6 convolution_convert_fusion
  466.6 3.5 multiply_reduce_fusion
  481.2 4.1 convolution_bitcast_fusion.2
  485.4 4.3 pad_maximum_fusion.1
  489.7 12.1 %copy.260 = f32[4,768,768]{2,0,1:T(4,128)} copy(f32[4,768,768]{1,2,0:T(8,128)} %pad_maximum_fusion.1) | data formatting | bytes 18874368 | tf_op jit(solution)/shard_map/concatenate | solution.py:170
  502.5 6.2 fusion.43
  509.7 2.5 convolution_bitcast_fusion.4
  514.8 2.8 fusion.42
  519.7 12.0 %convolution_bitcast_fusion.1 = f32[192,1,16,1536]{3,0,2,1:T(8,128)} fusion(bf16[64,16,1536]{2,0,1:T(8,128)(2,1)} %all-gather.16.cloned.1.call-done, bf16[64,16,192]{2,0,1:T(8,128)(2,1)S(1)} %all_gather.51), kind=kOutput, calls=%fused_computation.10 | convolution fusion | flops 603979776 | bytes 22413312 | tf_op jit(solution)/shard_map/ned,nef->def/dot_general | solution.py:122
  531.7 106.0 %all-reduce.3.cloned.1.call-done = f32[4,768,768]{2,0,1:T(4,128)} async-done(((f32[4,768,768]{2,0,1:T(4,128)}), f32[4,768,768]{2,0,1:T(4,128)}) %all-reduce.3.cloned.1.call-update) | async-done | bytes 9437200
  639.1 29.2 %copy.279 = f32[4,96,768]{0,1,2:T(8,128)} copy(f32[4,96,768]{2,0,1:T(4,128)S(1)} %constant_dynamic-slice_fusion.4) | data formatting | bytes 2359296
  668.3 33.0 %reshape.124 = f32[768,384]{1,0:T(8,128)} reshape(f32[768,96,4]{2,1,0:T(8,128)} %bitcast.198) | data formatting | bytes 2359296
  701.7 11.4 %convolution_bitcast_fusion = f32[192,1,16,1536]{3,0,2,1:T(8,128)} fusion(bf16[64,16,1536]{2,0,1:T(8,128)(2,1)} %all-gather.12.cloned.1.call-done, bf16[64,16,192]{2,0,1:T(8,128)(2,1)S(1)} %all_gather.56), kind=kOutput, calls=%fused_computation.9 | convolution fusion | flops 603979776 | bytes 22413312 | tf_op jit(solution)/shard_map/ned,nef->def/dot_general | solution.py:123
  713.1 15.2 %pad_maximum_fusion = f32[192,2,16,1536]{3,0,2,1:T(8,128)S(1)} fusion(f32[192,1,16,1536]{3,0,2,1:T(8,128)} %convolution_bitcast_fusion, f32[192,1,16,1536]{3,0,2,1:T(8,128)} %convolution_bitcast_fusion.1), kind=kLoop, calls=%fused_computation.5 | loop fusion | flops 9437184 | bytes 75497472 | tf_op jit(solution)/shard_map/stack | solution.py:124
  728.3 45.4 %copy.264 = f32[192,2,16,1536]{3,2,1,0:T(8,128)} copy(f32[192,2,16,1536]{3,0,2,1:T(8,128)S(1)} %pad_maximum_fusion) | data formatting | bytes 75497472
  773.8 2.7 convert_reduce_fusion
  776.4 5.3 all_gather.59
  783.2 12.1 %psum.7 = f32[4,96]{1,0:T(4,128)S(1)} all-reduce(f32[4,96]{1,0:T(4,128)S(1)} %copy.278), channel_id=1, replica_groups=mesh['shard'=4,'heads'=4,'tensor'=2] {'heads'}, use_global_device_ids=true, to_apply=%region_26.27 | all-reduce | flops 384 | bytes 3072 | tf_op jit(solution)/shard_map/psum | solution.py:176
  797.4 3.6 copy.261
  801.0 18.7 %all-gather.18.cloned.1.call-done = bf16[8,197,768]{2,1,0:T(8,128)(2,1)} async-done(((bf16[2,197,768]{2,1,0:T(8,128)(2,1)}), bf16[8,197,768]{2,1,0:T(8,128)(2,1)}) %all-gather.18.cloned.1.call-update) | async-done | bytes 2420752 | tf_op jit(solution)/shard_map/all_gather | solution.py:169
  819.6 3.6 copy.262
  823.2 26.8 %reduce-scatter.27.cloned.1.call-done = f32[192,384]{1,0:T(8,128)} async-done(((f32[768,384]{1,0:T(8,128)}), f32[192,384]{1,0:T(8,128)}) %reduce-scatter.27.cloned.1.call-update) | async-done | bytes 294928
  850.0 12.1 %reshape.125 = f32[192,96,4]{2,1,0:T(8,128)} reshape(f32[192,384]{1,0:T(8,128)} %reduce-scatter.27.cloned.1.call-done) | data formatting | bytes 589824
  862.1 7.2 copy.263
  (200 shorter events, 72.4 us)
Async XLA Ops:
  7.2 76.9 %copy-start = (bf16[8,197,768]{2,0,1:T(8,128)(2,1)S(1)}, bf16[8,197,768]{2,0,1:T(8,128)(2,1)}, u32[]{:S(2)}) copy-start(bf16[8,197,768]{2,0,1:T(8,128)(2,1)} %param.9) | copy-start | bytes 7262212
  7.2 78.1 %all-gather.10.cloned.1.call-start = ((), (), s32[]{:S(2)}) async-start(), calls=%async_computation.16 | async-start | bytes 5308416 | tf_op jit(solution)/shard_map/all_gather | solution.py:62
  8.5 22.7 %copy-start.34 = (bf16[2,96]{1,0:T(2,128)(2,1)S(1)}, bf16[2,96]{1,0:T(2,128)(2,1)}, u32[]{:S(2)}) copy-start(bf16[2,96]{1,0:T(2,128)(2,1)} %param.10) | copy-start | bytes 1156
  8.5 34.6 %copy-start.35 = (bf16[2,96]{1,0:T(2,128)(2,1)S(1)}, bf16[2,96]{1,0:T(2,128)(2,1)}, u32[]{:S(2)}) copy-start(bf16[2,96]{1,0:T(2,128)(2,1)} %param.11) | copy-start | bytes 1156
  8.5 46.2 %copy-start.28 = (bf16[96,16]{0,1:T(8,128)(2,1)S(1)}, bf16[96,16]{0,1:T(8,128)(2,1)}, u32[]{:S(2)}) copy-start(bf16[96,16]{0,1:T(8,128)(2,1)} %param.13) | copy-start | bytes 9220
  84.0 19.4 %copy-start.12 = (bf16[768,64,1]{0,1,2:T(8,128)(2,1)}, bf16[768,64,1]{0,1,2:T(8,128)(2,1)S(1)}, u32[]{:S(2)}) copy-start(bf16[768,64,1]{0,1,2:T(8,128)(2,1)S(1)} %reshape.116) | copy-start | bytes 294916
  84.1 5.0 copy-start.20
  84.1 5.0 copy-start.30
  84.7 15.5 %copy-start.2 = (bf16[2,197,768]{2,0,1:T(2,128)(2,1)}, bf16[2,197,768]{2,0,1:T(2,128)(2,1)S(1)}, u32[]{:S(2)}) copy-start(bf16[2,197,768]{2,0,1:T(2,128)(2,1)S(1)} %constant_dynamic-slice_fusion.3) | copy-start | bytes 1815556
  84.9 4.2 copy-start.18
  85.3 3.8 copy-start.25
  90.3 6.9 copy-start.5
  92.0 5.3 copy-start.7
  93.2 4.1 copy-start.13
  100.3 2.5 copy-start.16
  103.4 13.2 %copy-start.9 = (bf16[2,197,768]{2,1,0:T(8,128)(2,1)}, bf16[2,197,768]{2,1,0:T(8,128)(2,1)S(1)}, u32[]{:S(2)}) copy-start(bf16[2,197,768]{2,1,0:T(8,128)(2,1)S(1)} %add_convert_fusion.1) | copy-start | bytes 1815556
  103.7 67.0 %copy-start.11 = (f32[2,197,64]{1,2,0:T(8,128)}, f32[2,197,64]{1,2,0:T(8,128)S(1)}, u32[]{:S(2)}) copy-start(f32[2,197,64]{1,2,0:T(8,128)S(1)} %fusion.94) | copy-start | bytes 302596
  104.5 0.6 copy-start.27
  120.0 18.0 %all-to-all-start.1 = ((bf16[4,2,12288]{2,1,0:T(2,128)(2,1)}), bf16[4,2,12288]{2,1,0:T(2,128)(2,1)S(1)}, u32[]{:S(2)}, u32[]{:S(2)}) async-start(bf16[4,2,12288]{2,1,0:T(2,128)(2,1)} %reshape.133), calls=%async_computation.1 | async-start | bytes 393216 | tf_op jit(solution)/shard_map/all_to_all | solution.py:38
  123.4 131.0 %reduce-scatter.15.cloned.1.call-start = ((), (), s32[]{:S(2)}) async-start(), calls=%async_computation.17 | async-start | bytes 7864320 | tf_op jit(solution)/shard_map/reduce_scatter | solution.py:100
  167.6 127.8 %reduce-scatter.19.cloned.1.call-start = ((), (), s32[]{:S(2)}) async-start(), calls=%async_computation.21 | async-start | bytes 7864320 | tf_op jit(solution)/shard_map/reduce_scatter | solution.py:100
  169.9 22.4 %copy-start.10 = (bf16[2,197,768]{2,0,1:T(2,128)(2,1)}, bf16[2,197,768]{2,0,1:T(2,128)(2,1)S(1)}, u32[]{:S(2)}) copy-start(bf16[2,197,768]{2,0,1:T(2,128)(2,1)S(1)} %constant_dynamic-slice_fusion.2) | copy-start | bytes 1815556
  239.4 0.7 copy-start.24
  239.5 91.8 %all-gather.12.cloned.1.call-start = ((), (), s32[]{:S(2)}) async-start(), calls=%async_computation.18 | async-start | bytes 3932160 | tf_op jit(solution)/shard_map/all_gather | solution.py:103
  295.3 6.0 copy-start.4
  302.5 0.7 copy-start.29
  302.5 59.3 %all-gather.16.cloned.1.call-start = ((), (), s32[]{:S(2)}) async-start(), calls=%async_computation.22 | async-start | bytes 3932160 | tf_op jit(solution)/shard_map/all_gather | solution.py:103
  303.1 81.7 %reduce-scatter.17.cloned.1.call-start = ((), (), s32[]{:S(2)}) async-start(), calls=%async_computation.19 | async-start | bytes 1572864 | tf_op jit(solution)/shard_map/reduce_scatter | solution.py:43
  342.2 65.8 %reduce-scatter.21.cloned.1.call-start = ((), (), s32[]{:S(2)}) async-start(), calls=%async_computation.23 | async-start | bytes 1572864 | tf_op jit(solution)/shard_map/reduce_scatter | solution.py:43
  386.9 23.2 %all-to-all-start.2 = ((bf16[32,16,192]{2,1,0:T(8,128)(2,1)}), bf16[32,16,192]{2,1,0:T(8,128)(2,1)S(1)}, u32[]{:S(2)}, u32[]{:S(2)}) async-start(bf16[32,16,192]{2,1,0:T(8,128)(2,1)} %copy.238), calls=%async_computation.4 | async-start | bytes 524288 | tf_op jit(solution)/shard_map/all_to_all | solution.py:44
  410.1 9.4 %all-to-all-start.6 = ((bf16[32,16,192]{2,1,0:T(8,128)(2,1)}), bf16[32,16,192]{2,1,0:T(8,128)(2,1)S(1)}, u32[]{:S(2)}, u32[]{:S(2)}) async-start(bf16[32,16,192]{2,1,0:T(8,128)(2,1)} %copy.248), calls=%async_computation.10 | async-start | bytes 524288 | tf_op jit(solution)/shard_map/all_to_all | solution.py:44
  419.5 11.9 %all-to-all-start.3 = ((bf16[8,16,768]{2,1,0:T(8,128)(2,1)}), bf16[8,16,768]{2,1,0:T(8,128)(2,1)S(1)}, u32[]{:S(2)}, u32[]{:S(2)}) async-start(bf16[8,16,768]{2,1,0:T(8,128)(2,1)} %all_to_all.103), calls=%async_computation.5 | async-start | bytes 393216 | tf_op jit(solution)/shard_map/all_to_all | solution.py:45
  431.4 9.6 %all-to-all-start.7 = ((bf16[8,16,768]{2,1,0:T(8,128)(2,1)}), bf16[8,16,768]{2,1,0:T(8,128)(2,1)S(1)}, u32[]{:S(2)}, u32[]{:S(2)}) async-start(bf16[8,16,768]{2,1,0:T(8,128)(2,1)} %all_to_all.116), calls=%async_computation.11 | async-start | bytes 393216 | tf_op jit(solution)/shard_map/all_to_all | solution.py:45
  434.8 202.9 %all-reduce.3.cloned.1.call-start = ((), (), s32[]{:S(2)}) async-start(), calls=%async_computation.29 | async-start | bytes 18874368
  452.9 1.9 copy-start.17
  462.0 4.6 copy-start.14
  462.0 4.6 copy-start.15
  462.0 8.1 slice-start
  466.6 3.5 slice-start.1
  470.1 1.1 copy-start.8
  471.3 1.8 copy-start.6
  476.7 4.5 copy-start.19
  476.7 4.5 copy-start.21
  476.7 4.5 copy-start.26
  476.7 4.5 copy-start.31
  481.2 4.1 copy-start.3
  501.8 0.7 copy-start.23
  501.8 0.7 copy-start.22
  501.8 280.5 %reduce-scatter.25.cloned.1.call-start = ((), (), s32[]{:S(2)}) async-start(), calls=%async_computation.26 | async-start | bytes 442368
  509.7 285.6 %reduce-scatter.29.cloned.1.call-start = ((), (), s32[]{:S(2)}) async-start(), calls=%async_computation.28 | async-start | bytes 442368
  512.3 2.4 copy-start.33
  512.3 2.4 copy-start.32
  512.3 285.1 %all-gather.14.cloned.1.call-start = ((), (), s32[]{:S(2)}) async-start(), calls=%async_computation.20 | async-start | bytes 3072000 | tf_op jit(solution)/shard_map/all_gather | solution.py:116
  514.6 305.0 %all-gather.18.cloned.1.call-start = ((), (), s32[]{:S(2)}) async-start(), calls=%async_computation.24 | async-start | bytes 3072000 | tf_op jit(solution)/shard_map/all_gather | solution.py:169
  514.7 2.9 copy-start.36
  517.6 332.5 %reduce-scatter.27.cloned.1.call-start = ((), (), s32[]{:S(2)}) async-start(), calls=%async_computation.27 | async-start | bytes 1474560
  701.3 169.1 %reduce-scatter.23.cloned.1.call-start = ((), (), s32[]{:S(2)}) async-start(), calls=%async_computation.25 | async-start | bytes 40960 | tf_op jit(solution)/shard_map/reduce_scatter | solution.py:174
  862.1 8.3 copy-start.1
Sparse Core Ops, SparseCore 0:
  31.3 38.2 all-gather.9
  167.7 58.9 reduce-scatter.14
  239.6 55.7 reduce-scatter.18
  302.7 28.5 all-gather.11
  333.2 28.5 all-gather.15
  364.5 20.3 reduce-scatter.16
  387.7 20.2 reduce-scatter.20
  502.0 135.7 all-reduce.2
  641.6 33.8 reduce-scatter.24
  678.8 33.8 reduce-scatter.28
  714.9 52.0 all-gather.13
  768.5 51.0 all-gather.17
  822.1 27.9 reduce-scatter.26
  852.8 17.6 reduce-scatter.22

commit v2 on v1

--- a/solution.py
+++ b/solution.py
@@ -3,14 +3,372 @@
 import jax
 import jax.numpy as jnp
 from jax import lax
+from jax.experimental import pallas as pl
+from jax.experimental.pallas import tpu as pltpu
 from jax.sharding import PartitionSpec as P
 
 HEAD_DIM = 64
 F32 = jnp.float32
 BF16 = jnp.bfloat16
 ROWS = ("shard", "tensor")
+MESH = pl.DeviceIdType.MESH
+VMEM_BYTES = 58 * 1024 * 1024
 epsilon = 1e-06
 einsum = partial(jnp.einsum, preferred_element_type=F32)
+
+
+def dot(a, b):
+    return lax.dot_general(a, b, (((1,), (0,)), ((), ())), preferred_element_type=F32)
+
+
+def dot_t(a, b):
+    return lax.dot_general(a, b, (((1,), (1,)), ((), ())), preferred_element_type=F32)
+
+
+def swap_matrix(n):
+    out = lax.broadcasted_iota(jnp.int32, (n * n, n * n), 0)
+    row = lax.broadcasted_iota(jnp.int32, (n * n, n * n), 1)
+    return ((out // n == row % n) & (out % n == row // n)).astype(F32).astype(BF16)
+
+
+class Peers:
+    def __init__(self, sizes):
+        self.sizes = sizes
+        self.at = tuple(lax.axis_index(name) for name in ("shard", "heads", "tensor"))
+        self.count = sizes[0] * sizes[1] * sizes[2]
+
+    def flat(self, place):
+        return (place[0] * self.sizes[1] + place[1]) * self.sizes[2] + place[2]
+
+    def step(self, k, sign):
+        _, n_h, n_t = self.sizes
+        steps = (k // (n_h * n_t), (k // n_t) % n_h, k % n_t)
+        return tuple(
+            lax.rem(at + n + sign * d, n) for at, n, d in zip(self.at, self.sizes, steps)
+        )
+
+    def greet_all(self):
+        barrier = pltpu.get_barrier_semaphore()
+
+        def signal(k, carry):
+            pl.semaphore_signal(barrier, inc=1, device_id=self.step(k, 1), device_id_type=MESH)
+            return carry
+
+        lax.fori_loop(1, self.count, signal, 0)
+        pl.semaphore_wait(barrier, self.count - 1)
+
+
+def remote(src, dst, send, recv, place):
+    return pltpu.make_async_remote_copy(
+        src_ref=src, dst_ref=dst, send_sem=send, recv_sem=recv, device_id=place, device_id_type=MESH
+    )
+
+
+def expert_kernel(sizes, backward, *refs):
+    if backward:
+        (blocks, weights, gate, output, slots_out, act_out, back_out, bias_out, gathered,
+         w_a, w_b, gate_v, sums, slots, act, core_out, core_in, x_out, x_in, land, leave, back, land_back,
+         w_sem, o_sem, in_sems, back_sems, core_sems, x_sems, act_sems, g_sems, b_sems,
+         bias_all, bias_send, bias_land) = refs
+    else:
+        (blocks, weights, gate, slots_out, act_out, gate_out, back_out,
+         w_a, w_b, sums, slots, act, core_out, core_in, x_out, x_in, land, leave, back, land_back,
+         w_sem, o_sem, in_sems, back_sems, core_sems, x_sems, act_sems) = refs
+    peers = Peers(sizes)
+    s, h, t = peers.at
+    n_s, n_h, n_t = sizes
+    me = peers.flat(peers.at)
+    core, chip = lax.rem(s, 2), s // 2
+    sibling = (s + 1 - 2 * core, h, t)
+    across = (lax.rem(s + 2, n_s), h, t)
+    half = act.shape[0] // 2
+    own, other = core * half, (1 - core) * half
+    n_blocks = peers.count
+    first = 1 if backward else 0
+    loads = [
+        pltpu.make_async_copy(weights.at[first], w_a, w_sem.at[0]),
+        pltpu.make_async_copy(weights.at[1 - first], w_b, w_sem.at[1]),
+    ]
+    for load in loads:
+        load.start()
+    if backward:
+        gate_load = pltpu.make_async_copy(gate, gate_v, o_sem.at[0])
+        gate_load.start()
+    peers.greet_all()
+
+    def block_out(k):
+        place = peers.step(k, 1)
+        return remote(
+            blocks.at[place[1], place[0]], land.at[me], in_sems.at[0, k], in_sems.at[1, k], place
+        )
+
+    def block_in(k):
+        source = peers.flat(peers.step(k, -1))
+        return remote(
+            blocks.at[0, 0], land.at[source], in_sems.at[0, k], in_sems.at[1, k], sibling
+        )
+
+    def each(function, count=n_blocks, start=1):
+        lax.fori_loop(start, count, lambda k, carry: (function(k), carry)[1], 0)
+
+    each(lambda k: block_out(k).start())
+    land[me] = blocks[h, s]
+    swap = swap_matrix(16)
+    each(lambda k: block_in(k).wait_recv())
+    group = 8
+    for b in range(n_blocks // group):
+        rows = land[b * group : (b + 1) * group].reshape(group * 32, land.shape[2])
+        turned = dot(swap, rows).astype(BF16)
+        slots[:, b * 16 : (b + 1) * 16, :] = turned.reshape(16, 16, land.shape[2])
+    if backward:
+        g_copies = []
+        own_rows = output.shape[0]
+        mine = gathered.at[pl.ds(h * own_rows, own_rows)]
+        for d in range(1, n_h):
+            g_copies.append(
+                remote(output, mine, g_sems.at[0, d], g_sems.at[1, d], (s, lax.rem(h + d, n_h), t))
+            )
+        for copy in g_copies:
+            copy.start()
+        g_own = pltpu.make_async_copy(output, mine, g_sems.at[0, 0])
+        g_own.start()
+    loads[0].wait()
+
+    def core_copy(j):
+        return remote(
+            core_out.at[j], core_in.at[j], core_sems.at[0, j], core_sems.at[1, j], sibling
+        )
+
+    def x_copy(j):
+        return remote(x_out.at[j], x_in.at[j], x_sems.at[0, j], x_sems.at[1, j], across)
+
+    def act_copy(j):
+        return remote(
+            act.at[own + j], act.at[own + j], act_sems.at[0, j], act_sems.at[1, j], sibling
+        )
+
+    def act_in(j):
+        return remote(
+            act.at[other + j], act.at[other + j], act_sems.at[0, j], act_sems.at[1, j], sibling
+        )
+
+    def meet(j):
+        core_copy(j).wait_recv()
+        sums[j] = sums[j] + core_in[j].astype(F32)
+        x_out[j] = sums[j].astype(BF16)
+        x_copy(j).start()
+
+    def first_sums(j):
+        core_out[j] = dot(slots[other + j], w_a[other + j]).astype(BF16)
+        core_copy(j).start()
+        sums[j] = dot(slots[own + j], w_a[own + j])
+
+        @pl.when(j > 0)
+        def _():
+            meet(j - 1)
+
+    each(first_sums, half, 0)
+    meet(half - 1)
+    loads[1].wait()
+    if backward:
+        gate_load.wait()
+
+    def second(e):
+        leave[e] = dot_t(act[e], w_b[e]).astype(BF16)
+
+    def finish(j):
+        x_copy(j).wait_recv()
+        value = sums[j] + x_in[j].astype(F32)
+        if backward:
+            act[own + j] = (value * gate_v[j]).astype(BF16)
+        else:
+            value = value + gate[own + j]
+            cumulative = 0.5 + 0.5 * lax.erf(value * 0.7071067811865476)
+            act[own + j] = (value * cumulative).astype(BF16)
+            sums[j] = cumulative + value * (
+                jnp.exp(value * value * -0.5) * 0.3989422804014327
+            )
+        act_copy(j).start()
+        second(own + j)
+
+        @pl.when(j > 0)
+        def _():
+            act_in(j - 1).wait_recv()
+            second(other + j - 1)
+
+    each(finish, half, 0)
+    act_in(half - 1).wait_recv()
+    second(other + half - 1)
+
+    for b in range(n_blocks // group):
+        rows = leave[:, b * 16 : (b + 1) * 16, :].reshape(group * 32, leave.shape[2])
+        turned = dot(swap, rows).astype(BF16)
+        back[b * group : (b + 1) * group] = turned.reshape(group, 32, leave.shape[2])
+
+    def back_copy(k):
+        place = peers.step(k, 1)
+        return remote(
+            back.at[peers.flat(place)], land_back.at[me], back_sems.at[0, k], back_sems.at[1, k],
+            place,
+        )
+
+    def back_in(k):
+        source = peers.flat(peers.step(k, -1))
+        return remote(
+            back.at[0], land_back.at[source], back_sems.at[0, k], back_sems.at[1, k], sibling
+        )
+
+    each(lambda k: back_copy(k).start())
+    land_back[me] = back[me]
+    stores = [pltpu.make_async_copy(act, act_out, o_sem.at[1])]
+    if not backward:
+        stores.append(pltpu.make_async_copy(sums, gate_out, o_sem.at[0]))
+    for store in stores:
+        store.start()
+    slots_out[...] = slots[...]
+    if backward:
+        across_t = (s, h, 1 - t)
+        width = bias_out.shape[1]
+
+        def bias_row(e):
+            bias_all[pl.ds(e, 1), :] = jnp.sum(act[e].astype(F32), axis=0, keepdims=True)
+
+        each(bias_row, 2 * half, 0)
+
+        def piece(for_t):
+            return bias_all[:, pl.ds(pl.multiple_of((core * n_t + for_t) * width, 128), width)]
+
+        bias_send[...] = piece(1 - t)
+        bias_copy = remote(bias_send, bias_land, b_sems.at[0], b_sems.at[1], across_t)
+        bias_copy.start()
+        bias_copy.wait()
+        bias_out[...] = jnp.where(t == chip, piece(t), bias_land[...])
+    each(lambda k: back_in(k).wait_recv())
+    back_out[...] = land_back[...]
+    for store in stores:
+        store.wait()
+    if backward:
+        for copy in g_copies:
+            copy.wait()
+        g_own.wait()
+    each(lambda k: block_out(k).wait_send())
+    each(lambda k: back_copy(k).wait_send())
+    for copy in (core_copy, x_copy, act_copy):
+        each(lambda j: copy(j).wait_send(), half, 0)
+
+
+def expert_pass(sizes, backward, blocks, weights, gate, output=None, bias_width=0):
+    _, experts, rows, hidden = weights.shape
+    devices = sizes[0] * sizes[1] * sizes[2]
+    images = 2 * devices
+    half = experts // 2
+    vmem = pl.BlockSpec(memory_space=pltpu.VMEM)
+    hbm = pl.BlockSpec(memory_space=pl.ANY)
+    slots = jax.ShapeDtypeStruct((experts, images, rows), BF16)
+    act = jax.ShapeDtypeStruct((experts, images, hidden), BF16)
+    gate_shape = (half, images, hidden)
+    returned = jax.ShapeDtypeStruct((devices, 2 * experts, rows), BF16)
+    if backward:
+        operands, in_specs = (blocks, weights, gate, output), [vmem, hbm, hbm, hbm]
+        gathered = (sizes[1] * output.shape[0], *output.shape[1:])
+        outs = (
+            slots, act, returned, jax.ShapeDtypeStruct((experts, bias_width), F32),
+            jax.ShapeDtypeStruct(gathered, BF16),
+        )
+        out_specs = (vmem, hbm, vmem, vmem, hbm)
+    else:
+        operands, in_specs = (blocks, weights, gate), [vmem, hbm, vmem]
+        outs = (slots, act, jax.ShapeDtypeStruct(gate_shape, F32), returned)
+        out_specs = (vmem, hbm, hbm, vmem)
+    weight = pltpu.VMEM((experts, rows, hidden), BF16)
+    chunk = pltpu.VMEM((half, images, hidden), BF16)
+    block = pltpu.VMEM((devices, 2 * experts, rows), BF16)
+    dma = pltpu.SemaphoreType.DMA
+    scratch = [weight, weight]
+    if backward:
+        scratch.append(pltpu.VMEM(gate_shape, F32))
+    scratch += [
+        pltpu.VMEM(gate_shape, F32),
+        pltpu.VMEM(slots.shape, BF16),
+        pltpu.VMEM(act.shape, BF16),
+        chunk, chunk, chunk, chunk, block,
+        pltpu.VMEM(slots.shape, BF16),
+        block, block,
+        dma((2,)), dma((2,)), dma((2, devices)), dma((2, devices)),
+        dma((2, half)), dma((2, half)), dma((2, half)),
+    ]
+    if backward:
+        scratch += [
+            dma((2, sizes[1])), dma((2,)),
+            pltpu.VMEM((experts, hidden), F32),
+            pltpu.VMEM((experts, bias_width), F32),
+            pltpu.VMEM((experts, bias_width), F32),
+        ]
+    return pl.pallas_call(
+        partial(expert_kernel, sizes, backward),
+        out_shape=outs,
+        in_specs=in_specs,
+        out_specs=out_specs,
+        scratch_shapes=scratch,
+        compiler_params=pltpu.CompilerParams(
+            collective_id=2 if backward else 1, has_side_effects=True, vmem_limit_bytes=VMEM_BYTES
+        ),
+        cost_estimate=pl.CostEstimate(
+            flops=8 * images * experts * rows * hidden,
+            bytes_accessed=weights.size * 2,
+            transcendentals=0,
+        ),
+        name="experts_back" if backward else "experts_ahead",
+    )(*operands)
+
+
+def weight_grad_kernel(slots_0, act_0, slots_1, act_1, out):
+    group = out.shape[2]
+    d_block = out.shape[0]
+    images, rows = slots_0.shape[1:]
+    g, first = pl.program_id(1), pl.program_id(2) * d_block
+    n = group * d_block
+    row = lax.broadcasted_iota(jnp.int32, (n, rows), 0)
+    column = lax.broadcasted_iota(jnp.int32, (n, rows), 1)
+    pick = (column == first + row // group).astype(F32).astype(BF16)
+    row = lax.broadcasted_iota(jnp.int32, (n, group * images), 0)
+    column = lax.broadcasted_iota(jnp.int32, (n, group * images), 1)
+    same = row % group == column // images
+
+    def term(slots, act):
+        lines = slots[pl.ds(g * group, group)].reshape(group * images, rows)
+        spread = jnp.where(same, dot_t(pick, lines), 0.0).astype(BF16)
+        values = act[pl.ds(g * group, group)].reshape(group * images, act.shape[2])
+        out[...] = dot(spread, values).reshape(out.shape)
+
+    @pl.when(pl.program_id(0) == 0)
+    def _():
+        term(slots_0, act_0)
+
+    @pl.when(pl.program_id(0) == 1)
+    def _():
+        term(slots_1, act_1)
+
+
+def weight_grads(slots_0, act_0, slots_1, act_1):
+    experts, images, rows = slots_0.shape
+    hidden = act_0.shape[2]
+    group, d_block = 8, 32
+    vmem = pl.BlockSpec(memory_space=pltpu.VMEM)
+    return pl.pallas_call(
+        weight_grad_kernel,
+        grid=(2, experts // group, rows // d_block),
+        out_shape=jax.ShapeDtypeStruct((rows, 2, experts, hidden), F32),
+        in_specs=[vmem] * 4,
+        out_specs=pl.BlockSpec((d_block, 1, group, hidden), lambda m, g, d: (d, m, g, 0)),
+        compiler_params=pltpu.CompilerParams(vmem_limit_bytes=VMEM_BYTES),
+        cost_estimate=pl.CostEstimate(
+            flops=4 * images * experts * rows * hidden,
+            bytes_accessed=8 * rows * experts * hidden,
+            transcendentals=0,
+        ),
+        name="weight_grads",
+    )(slots_0, act_0, slots_1, act_1)
 
 
 def normalize(values, scale, shift):
@@ -39,6 +397,20 @@
     return lax.all_gather(slots, "tensor", axis=0, tiled=True)
 
 
+def to_blocks(slots, sizes):
+    own, experts, width = slots.shape
+    n_s, n_h, _ = sizes
+    slots = slots.reshape(own, n_h, experts // n_h, n_s, width // n_s)
+    return slots.transpose(1, 3, 0, 2, 4).reshape(n_h, n_s, own * experts // n_h, width // n_s)
+
+
+def from_blocks(blocks, sizes):
+    n_s, n_h, n_t = sizes
+    rows = blocks.shape[2]
+    blocks = jnp.sum(blocks.reshape(n_s, n_h, n_t, 2, -1, rows).astype(F32), axis=2)
+    return blocks.transpose(2, 1, 3, 0, 4).reshape(2, -1, n_s * rows)
+
+
 def to_images(slots):
     slots = lax.psum_scatter(slots, "tensor", scatter_dimension=0, tiled=True)
     slots = lax.all_to_all(slots, "shard", split_axis=0, concat_axis=2, tiled=True)
@@ -47,6 +419,9 @@
 
 def shards(tokens, norm_scales, norm_biases, w_attn, phi, experts, in_bias, out_bias, cotangent):
     heads_n = lax.axis_size("heads")
+    sizes = tuple(lax.axis_size(name) for name in ("shard", "heads", "tensor"))
+    if sizes != (4, 4, 2) or tokens.shape[0] != 8 or experts.shape[2] != 16:
+        sizes = None
     group, seq_len, width = tokens.shape
     own = group // heads_n
     heads_index = lax.axis_index("heads")
@@ -66,7 +441,7 @@
         lax.all_gather(phi, "heads", axis=1, tiled=True), ROWS, axis=0, tiled=True
     )
     out_rows = lax.all_gather(out_bias, "tensor", axis=1, tiled=True).astype(F32)
-    e_own = experts.shape[2] // lax.axis_size("shard") if experts.shape[2] % lax.axis_size("shard") == 0 else 0
+    e_own = experts.shape[2] // lax.axis_size("shard")
     in_local = lax.dynamic_slice_in_dim(in_full, tensor_index * hidden, hidden, 1)
     factor = HEAD_DIM ** (-0.5)
     tokens = lax.dynamic_slice_in_dim(tokens, heads_index * own, own, 0)
@@ -93,44 +468,65 @@
     dispatch_b = dispatch.astype(BF16)
     combine = jax.nn.softmax(logits, axis=2)
     combine_b = combine.astype(BF16)
-    slot_in = to_experts(einsum("nse,nsd->ned", dispatch_b, normed_two_b).astype(BF16))
-    share = 1 if e_own else 0
-
-    def meet(partial_sum):
-        return lax.psum_scatter(partial_sum, "shard", scatter_dimension=share, tiled=True)
-
-    def spread(values):
-        return lax.all_gather(values, "shard", axis=share, tiled=True)
-
-    pre = meet(einsum("ned,def->nef", slot_in, experts[:, 0]))
-    if e_own:
-        pre = pre + lax.dynamic_slice_in_dim(in_local, shard_index * e_own, e_own, 0)
+    slot_in = einsum("nse,nsd->ned", dispatch_b, normed_two_b).astype(BF16)
+    if sizes is not None:
+        turned = jnp.transpose(experts, (1, 2, 0, 3))
+        slot_in, activated, gate, back = expert_pass(
+            sizes, False, to_blocks(slot_in, sizes), turned, in_local[:, None, :]
+        )
+        out_all = lax.all_gather(
+            lax.all_gather(out_bias, "heads", axis=0, tiled=True), ROWS, axis=1, tiled=True
+        )
+        slot_out = (from_blocks(back, sizes) + out_all.astype(F32)).astype(BF16)
     else:
-        pre = pre + in_local
-    gelu_value, gelu_back = jax.vjp(partial(jax.nn.gelu, approximate=False), pre)
-    activated = spread(gelu_value.astype(BF16))
-    slot_out_part = einsum("nef,def->ned", activated, experts[:, 1])
-    slot_out_part = slot_out_part + jnp.where(tensor_index == 0, out_rows, 0.0)
-    slot_out = to_images(slot_out_part).astype(BF16)
+        slot_in = to_experts(slot_in)
+        share = 1 if e_own else 0
+
+        def meet(partial_sum):
+            return lax.psum_scatter(partial_sum, "shard", scatter_dimension=share, tiled=True)
+
+        def spread(values):
+            return lax.all_gather(values, "shard", axis=share, tiled=True)
+
+        pre = meet(einsum("ned,def->nef", slot_in, experts[:, 0]))
+        if e_own:
+            pre = pre + lax.dynamic_slice_in_dim(in_local, shard_index * e_own, e_own, 0)
+        else:
+            pre = pre + in_local
+        gelu_value, gelu_back = jax.vjp(partial(jax.nn.gelu, approximate=False), pre)
+        activated = spread(gelu_value.astype(BF16))
+        slot_out_part = einsum("nef,def->ned", activated, experts[:, 1])
+        slot_out_part = slot_out_part + jnp.where(tensor_index == 0, out_rows, 0.0)
+        slot_out = to_images(slot_out_part).astype(BF16)
     output = (hidden_one + einsum("nse,ned->nsd", combine_b, slot_out)).astype(BF16)
-    output = lax.all_gather(output, "heads", axis=0, tiled=True)
     grad_combine = einsum("nsd,ned->nse", cotangent, slot_out)
-    grad_slot = to_experts(einsum("nse,nsd->ned", combine_b, cotangent).astype(BF16))
-    grad_act = meet(einsum("ned,def->nef", grad_slot, experts[:, 1]))
-    grad_pre = spread(gelu_back(grad_act)[0].astype(BF16))
-    grad_slot_in = einsum("nef,def->ned", grad_pre, experts[:, 0]).astype(BF16)
-    input_term = einsum("ned,nef->def", slot_in, grad_pre)
-    output_term = einsum("ned,nef->def", grad_slot, activated)
-    experts_grad = jnp.stack((input_term, output_term), axis=1)
-    grad_slot_in = to_images(grad_slot_in.astype(F32)).astype(BF16)
-    in_bias_grad = lax.dynamic_slice_in_dim(
-        lax.all_gather(jnp.sum(grad_pre.astype(F32), axis=0), "tensor", axis=1, tiled=True),
-        (shard_index * lax.axis_size("tensor") + tensor_index) * in_bias.shape[1],
-        in_bias.shape[1],
-        1,
-    )
+    grad_slot = einsum("nse,nsd->ned", combine_b, cotangent).astype(BF16)
+    if sizes is not None:
+        grad_slot, grad_pre, back, in_bias_grad, output = expert_pass(
+            sizes, True, to_blocks(grad_slot, sizes), turned, gate, output, in_bias.shape[1]
+        )
+        grad_slot_in = from_blocks(back, sizes).astype(BF16)
+        experts_grad = weight_grads(slot_in, grad_pre, grad_slot, activated)
+        grad_slot_sum = jnp.sum(grad_slot.astype(F32), axis=1)
+    else:
+        output = lax.all_gather(output, "heads", axis=0, tiled=True)
+        grad_slot = to_experts(grad_slot)
+        grad_act = meet(einsum("ned,def->nef", grad_slot, experts[:, 1]))
+        grad_pre = spread(gelu_back(grad_act)[0].astype(BF16))
+        grad_slot_in = einsum("nef,def->ned", grad_pre, experts[:, 0]).astype(BF16)
+        input_term = einsum("ned,nef->def", slot_in, grad_pre)
+        output_term = einsum("ned,nef->def", grad_slot, activated)
+        experts_grad = jnp.stack((input_term, output_term), axis=1)
+        grad_slot_in = to_images(grad_slot_in.astype(F32)).astype(BF16)
+        in_bias_grad = lax.dynamic_slice_in_dim(
+            lax.all_gather(jnp.sum(grad_pre.astype(F32), axis=0), "tensor", axis=1, tiled=True),
+            (shard_index * lax.axis_size("tensor") + tensor_index) * in_bias.shape[1],
+            in_bias.shape[1],
+            1,
+        )
+        grad_slot_sum = jnp.sum(grad_slot.astype(F32), axis=0)
     out_bias_grad = lax.dynamic_slice_in_dim(
-        jnp.sum(grad_slot.astype(F32), axis=0),
+        grad_slot_sum,
         tensor_index * out_bias.shape[1],
         out_bias.shape[1],
         1,

time: 889 us -> 731 us (0.82)
  Pallas kernels: 0 us -> 190 us
  waiting for transfers between devices: 283 us -> 171 us
  matrix products: 135 us -> 51.3 us
  local copies, waits for them, and re-layouts: 214 us -> 154 us
  blocking collectives: 171 us -> 129 us
  other arithmetic: 39.2 us -> 14.6 us
  starting transfers between devices: 19.8 us -> 0.54 us
    pallas_call x0 -> x3, Pallas kernels: none -> 190 us  [the longest x2 162 us: expert_pass(): pl.pallas_call(partial(expert_kernel, sizes, backward), out_shape=outs, i...]
    dot_general x8 -> x2, matrix products: 79.7 us -> 2.66 us  [the longest x1 1.4 us: shards(): slot_in = einsum('nse,nsd->ned', dispatch_b, normed_two_b).astype(BF16)]
    reduce_scatter x4 -> x0, waiting for transfers between devices: 70.8 us -> none  [the longest x2 41 us: meet(): lax.psum_scatter(partial_sum, 'shard', scatter_dimension=share, tiled=True)]
    all_to_all x3 -> x0, blocking collectives: 43.3 us -> none  [the longest x2 31.5 us: to_experts(): lax.all_to_all(slots, 'heads', split_axis=1, concat_axis=0, tiled=True)]
    all_gather x3 -> x0, waiting for transfers between devices: 42.7 us -> none  [the longest x2 42.7 us: spread(): return lax.all_gather(values, 'shard', axis=share, tiled=True)]
    unnamed x96 -> x87, local copies, waits for them, and re-layouts: 151 us -> 119 us
    all_to_all x5 -> x0, starting transfers between devices: 18.1 us -> none  [the longest x2 7.97 us: to_images(): lax.all_to_all(slots, 'heads', split_axis=0, concat_axis=1, tiled=True)]
    unnamed x18 -> x11, waiting for transfers between devices: 134 us -> 151 us
  transfers between devices with their start and end apart: 19 -> 7, of which waited for: 12 -> 4; matrix products, arithmetic and copies ran while one was open for 31% -> 18% of each run, Pallas kernels for 0% -> 4%
where the time goes in v2:
time: 731 us; the launch traced here: 726 us
  Pallas kernels  190 us (26%)
  waiting for transfers between devices  171 us (23%)
  local copies, waits for them, and re-layouts  154 us (21%)
  blocking collectives  129 us (18%)
  matrix products  51.3 us (7%)
  between operations  15.7 us (2%)
  other arithmetic  14.6 us (2%)
    pallas_call x2, Pallas kernels, expert_pass(): pl.pallas_call(partial(expert_kernel, sizes, backward), out_shape=outs, i...  162 us
    unnamed x11, waiting for transfers between devices  151 us
    unnamed x87, local copies, waits for them, and re-layouts  119 us
    pallas_call x1, Pallas kernels, weight_grads(): pl.pallas_call(weight_grad_kernel, grid=(2, experts // group, rows // d_b...  27.4 us
    all_gather x1, blocking collectives, shards(): lax.all_gather(w_attn, 'heads', axis=2, tiled=True)  21.3 us
    all_gather x1, waiting for transfers between devices, shards(): input_grad = lax.all_gather(input_grad, 'heads', axis=0, tiled=True)  18.2 us
    all_gather x1, blocking collectives, shards(): lax.all_gather(lax.all_gather(out_bias, 'heads', axis=0, tiled=True), ROW...  16.3 us
    all_gather x1, blocking collectives, shards(): lax.all_gather(lax.all_gather(phi, 'heads', axis=1, tiled=True), ROWS, ax...  15.8 us
  transfers between devices with their start and end apart: 7, of which 4 were waited for; matrix products, arithmetic and copies ran while one was open for 18% of the time, Pallas kernels for 4%

profile of v2, /device:TPU:0, one launch (start us, length us, event | category | flops | bytes accessed | tf_op | source)
XLA Modules:
  0.0 726.0 jit_solution(1862779606773812475)
XLA Ops:
  7.2 1.2 copy.167
  8.5 21.3 %all_gather.32 = bf16[4,96,768]{1,0,2:T(4,128)(2,1)S(1)} all-gather(bf16[4,96,192]{1,0,2:T(4,128)(2,1)S(1)} %copy.167), channel_id=1, replica_groups=mesh['shard'=4,'heads'=4,'tensor'=2] {'heads'}, dimensions={2}, use_global_device_ids=true | all-gather | bytes 737280 | tf_op jit(solution)/shard_map/all_gather | solution.py:438
  29.8 1.2 copy.168
  31.1 11.8 %all-gather.1 = bf16[8,96,2]{1,2,0:T(2,128)(2,1)S(1)} all-gather(bf16[1,96,2]{1,2,0:T(2,128)(2,1)S(1)} %bitcast.159), channel_id=1, replica_groups=mesh['shard'=4,'heads'=4,'tensor'=2] {'shard','tensor'}, dimensions={0}, use_global_device_ids=true | all-gather | bytes 3456 | tf_op jit(solution)/shard_map/all_gather | solution.py:434
  43.0 11.5 %all-gather = bf16[8,96,2]{1,2,0:T(2,128)(2,1)S(1)} all-gather(bf16[1,96,2]{1,2,0:T(2,128)(2,1)S(1)} %bitcast.160), channel_id=1, replica_groups=mesh['shard'=4,'heads'=4,'tensor'=2] {'shard','tensor'}, dimensions={0}, use_global_device_ids=true | all-gather | bytes 3456 | tf_op jit(solution)/shard_map/all_gather | solution.py:433
  54.5 13.1 %all_gather.34 = bf16[96,64]{0,1:T(8,128)(2,1)S(1)} all-gather(bf16[96,16]{0,1:T(8,128)(2,1)S(1)} %copy-done.27), channel_id=1, replica_groups=mesh['shard'=4,'heads'=4,'tensor'=2] {'heads'}, dimensions={1}, use_global_device_ids=true | all-gather | bytes 15360 | tf_op jit(solution)/shard_map/all_gather | solution.py:441
  67.7 15.8 %all-gather.2 = bf16[8,96,64]{1,2,0:T(8,128)(2,1)S(1)} all-gather(bf16[1,96,64]{1,2,0:T(8,128)(2,1)S(1)} %bitcast.154), channel_id=1, replica_groups=mesh['shard'=4,'heads'=4,'tensor'=2] {'shard','tensor'}, dimensions={0}, use_global_device_ids=true | all-gather | bytes 110592 | tf_op jit(solution)/shard_map/all_gather | solution.py:440
  83.7 20.5 %copy.231 = bf16[192,2,16,1536]{3,0,2,1:T(8,128)(2,1)} copy(bf16[192,2,16,1536]{3,2,1,0:T(8,128)(2,1)} %param.14) | data formatting | bytes 37748736 | tf_op args[5]
  104.2 14.1 %all_gather.36 = bf16[16,3072]{1,0:T(8,128)(2,1)S(1)} all-gather(bf16[16,384]{1,0:T(8,128)(2,1)S(1)} %copy-done.24), channel_id=1, replica_groups=mesh['shard'=4,'heads'=4,'tensor'=2] {'shard','tensor'}, dimensions={1}, use_global_device_ids=true | all-gather | bytes 110592 | tf_op jit(solution)/shard_map/all_gather | solution.py:435
  119.0 13.1 %all_gather.37 = bf16[64,96]{1,0:T(8,128)(2,1)S(1)} all-gather(bf16[16,96]{1,0:T(8,128)(2,1)S(1)} %copy-done.28), channel_id=1, replica_groups=mesh['shard'=4,'heads'=4,'tensor'=2] {'heads'}, dimensions={0}, use_global_device_ids=true | all-gather | bytes 15360 | tf_op jit(solution)/shard_map/all_gather | solution.py:478
  132.2 16.3 %all-gather.3 = bf16[8,96,64]{1,2,0:T(8,128)(2,1)S(1)} all-gather(bf16[1,96,64]{1,2,0:T(8,128)(2,1)S(1)} %bitcast.155), channel_id=1, replica_groups=mesh['shard'=4,'heads'=4,'tensor'=2] {'shard','tensor'}, dimensions={0}, use_global_device_ids=true | all-gather | bytes 110592 | tf_op jit(solution)/shard_map/all_gather | solution.py:477
  150.0 2.3 constant_dynamic-slice_fusion.2
  152.9 3.8 convert_bitcast_fusion
  156.7 1.1 fusion.65
  157.8 1.2 copy.169
  159.0 1.3 copy.170
  160.3 2.6 copy.171
  162.9 5.2 fusion.67
  168.2 3.3 convolution_convert_fusion.1
  171.4 2.5 fusion.68
  177.1 1.4 convolution_convert_fusion.3
  179.6 73.9 %experts_ahead.1 = (bf16[16,64,192]{2,1,0:T(8,128)(2,1)}, bf16[16,64,1536]{2,1,0:T(8,128)(2,1)}, f32[8,64,1536]{2,1,0:T(8,128)}, bf16[32,32,192]{2,1,0:T(8,128)(2,1)}) custom-call(bf16[4,4,32,192]{3,2,1,0:T(8,128)(2,1)} %bitcast.143, bf16[2,16,192,1536]{3,2,1,0:T(8,128)(2,1)} %bitcast.126, f32[16,1,1536]{2,1,0:T(1,128)} %broadcast_in_dim.4.refs_2_), custom_call_target="tpu_custom_call" | custom-call | flops 2415919104 | bytes 18874368 | tf_op jit(solution)/shard_map/experts_ahead/pallas_call | solution.py:307
  253.5 1.2 convert_reduce_fusion.1
  255.3 1.3 convolution_convert_fusion.4
  256.6 2.2 fusion.18.refs_3_
  260.1 88.5 %experts_back.1 = (bf16[16,64,192]{2,1,0:T(8,128)(2,1)}, bf16[16,64,1536]{2,1,0:T(8,128)(2,1)}, bf16[32,32,192]{2,1,0:T(8,128)(2,1)}, f32[16,384]{1,0:T(8,128)}, bf16[8,197,768]{2,1,0:T(8,128)(2,1)}) custom-call(bf16[4,4,32,192]{3,2,1,0:T(8,128)(2,1)} %bitcast.142, bf16[2,16,192,1536]{3,2,1,0:T(8,128)(2,1)} %bitcast.127, ...), custom_call_target="tpu_custom_call" | custom-call | flops 2415919104 | bytes 18874368 | tf_op jit(solution)/shard_map/experts_back/pallas_call | solution.py:307
  348.7 1.2 reduce
  350.3 2.6 fusion.55
  352.8 1.8 fusion.38
  354.7 3.2 multiply_reduce_fusion.2
  357.8 1.7 multiply_add_fusion
  359.5 1.0 copy-done.2
  360.6 1.9 convolution_convert_fusion.2
  362.5 1.2 copy.182
  363.7 4.6 convolution_convert_fusion
  368.3 1.0 multiply_reduce_fusion
  369.4 1.0 multiply_convert_fusion
  370.5 0.9 multiply_convert_fusion.1
  371.6 1.5 multiply_convert_fusion.2
  373.1 2.2 convolution_bitcast_fusion.1
  375.4 2.2 copy.188
  377.6 1.1 copy.187
  378.7 2.3 copy.186
  381.1 3.8 convolution_bitcast_fusion
  384.8 4.3 pad_maximum_fusion
  389.2 12.1 %copy.191 = f32[4,768,768]{2,0,1:T(4,128)} copy(f32[4,768,768]{1,2,0:T(8,128)} %pad_maximum_fusion) | data formatting | bytes 18874368 | tf_op jit(solution)/shard_map/concatenate | solution.py:566
  401.6 5.5 fusion.26
  407.1 0.9 copy.205
  408.2 2.2 convolution_bitcast_fusion.2
  410.4 2.6 fusion.25
  414.3 124.3 %all-reduce.3.cloned.1.call-done = f32[4,768,768]{2,0,1:T(4,128)} async-done(((f32[4,768,768]{2,0,1:T(4,128)}), f32[4,768,768]{2,0,1:T(4,128)}) %all-reduce.3.cloned.1.call-update) | async-done | bytes 9437200
  538.7 1.3 constant_dynamic-slice_fusion.3
  540.0 29.2 %copy.207 = f32[4,96,768]{0,1,2:T(8,128)} copy(f32[4,96,768]{2,0,1:T(4,128)S(1)} %constant_dynamic-slice_fusion.3) | data formatting | bytes 2359296
  569.2 33.0 %reshape.145 = f32[768,384]{1,0:T(8,128)} reshape(f32[768,96,4]{2,1,0:T(8,128)} %bitcast.128) | data formatting | bytes 2359296
  602.4 3.7 copy.192
  606.8 27.4 %weight_grads.1 = f32[192,2,16,1536]{3,2,1,0:T(8,128)} custom-call(bf16[16,64,192]{2,1,0:T(8,128)(2,1)} %get-tuple-element.22.slots_0, bf16[16,64,1536]{2,1,0:T(8,128)(2,1)} %get-tuple-element.23.act_0, bf16[16,64,192]{2,1,0:T(8,128)(2,1)} %get-tuple-element.24.slots_1, bf16[16,64,1536]{2,1,0:T(8,128)(2,1)} %get-tuple-element.25.act_1), custom_call_target="tpu_custom_call" | custom-call | flops 1207959552 | bytes 37748736 | tf_op jit(solution)/shard_map/weight_grads/pallas_call | solution.py:358
  635.1 12.1 %psum.7 = f32[4,96]{1,0:T(4,128)S(1)} all-reduce(f32[4,96]{1,0:T(4,128)S(1)} %copy.206), channel_id=1, replica_groups=mesh['shard'=4,'heads'=4,'tensor'=2] {'heads'}, use_global_device_ids=true, to_apply=%region_24.0 | all-reduce | flops 384 | bytes 3072 | tf_op jit(solution)/shard_map/psum | solution.py:572
  647.1 1.5 copy.210
  649.2 18.2 %all-gather.9.cloned.1.call-done = bf16[8,197,768]{2,1,0:T(8,128)(2,1)} async-done(((bf16[2,197,768]{2,1,0:T(8,128)(2,1)}), bf16[8,197,768]{2,1,0:T(8,128)(2,1)}) %all-gather.9.cloned.1.call-update) | async-done | bytes 2420752 | tf_op jit(solution)/shard_map/all_gather | solution.py:565
  667.4 3.6 copy.193
  671.0 26.7 %reduce-scatter.15.cloned.1.call-done = f32[192,384]{1,0:T(8,128)} async-done(((f32[768,384]{1,0:T(8,128)}), f32[192,384]{1,0:T(8,128)}) %reduce-scatter.15.cloned.1.call-update) | async-done | bytes 294928
  697.7 12.1 %reshape.146 = f32[192,96,4]{2,1,0:T(8,128)} reshape(f32[192,384]{1,0:T(8,128)} %reduce-scatter.15.cloned.1.call-done) | data formatting | bytes 589824
  709.8 7.2 copy.194
  717.0 1.3 reduce-scatter.11.cloned.1.call-done
  (136 shorter events, 14.4 us)
Async XLA Ops:
  7.2 142.2 %copy-start = (bf16[8,197,768]{2,0,1:T(8,128)(2,1)S(1)}, bf16[8,197,768]{2,0,1:T(8,128)(2,1)}, u32[]{:S(2)}) copy-start(bf16[8,197,768]{2,0,1:T(8,128)(2,1)} %param.17) | copy-start | bytes 7262212
  7.2 145.7 %all-gather.7.cloned.1.call-start = ((), (), s32[]{:S(2)}) async-start(), calls=%async_computation.4 | async-start | bytes 5308416 | tf_op jit(solution)/shard_map/all_gather | solution.py:437
  29.8 1.3 copy-start.31
  29.8 13.2 %copy-start.32 = (bf16[2,96]{1,0:T(2,128)(2,1)S(1)}, bf16[2,96]{1,0:T(2,128)(2,1)}, u32[]{:S(2)}) copy-start(bf16[2,96]{1,0:T(2,128)(2,1)} %param.10) | copy-start | bytes 1156
  29.8 24.7 %copy-start.27 = (bf16[96,16]{0,1:T(8,128)(2,1)S(1)}, bf16[96,16]{0,1:T(8,128)(2,1)}, u32[]{:S(2)}) copy-start(bf16[96,16]{0,1:T(8,128)(2,1)} %param.13) | copy-start | bytes 9220
  31.0 507.6 %all-reduce.3.cloned.1.call-start = ((), (), s32[]{:S(2)}) async-start(), calls=%async_computation.10 | async-start | bytes 18874368
  83.6 90.9 %copy-start.13 = (bf16[768,64,1]{0,1,2:T(8,128)(2,1)}, bf16[768,64,1]{0,1,2:T(8,128)(2,1)S(1)}, u32[]{:S(2)}) copy-start(bf16[768,64,1]{0,1,2:T(8,128)(2,1)S(1)} %reshape.137) | copy-start | bytes 294916
  83.7 20.6 %copy-start.24 = (bf16[16,384]{1,0:T(8,128)(2,1)S(1)}, bf16[16,384]{1,0:T(8,128)(2,1)}, u32[]{:S(2)}) copy-start(bf16[16,384]{1,0:T(8,128)(2,1)} %param.15) | copy-start | bytes 36868
  83.7 35.4 %copy-start.28 = (bf16[16,96]{1,0:T(8,128)(2,1)S(1)}, bf16[16,96]{1,0:T(8,128)(2,1)}, u32[]{:S(2)}) copy-start(bf16[16,96]{1,0:T(8,128)(2,1)} %param.16) | copy-start | bytes 9220
  149.3 3.5 copy-start.22
  149.4 3.5 copy-start.29
  152.8 3.8 copy-start.25
  160.3 7.8 %copy-start.5 = (bf16[1,2,197,768]{2,3,1,0:T(8,128)(2,1)}, bf16[1,2,197,768]{2,3,1,0:T(8,128)(2,1)S(1)}, u32[]{:S(2)}) copy-start(bf16[1,2,197,768]{2,3,1,0:T(8,128)(2,1)S(1)} %copy.170) | copy-start | bytes 1815556
  171.4 2.5 copy-start.17
  174.5 0.8 copy-start.8
  175.7 3.9 copy-start.12
  255.3 1.3 copy-start.11
  349.8 3.0 copy-start.20
  352.8 1.8 copy-start.14
  359.5 1.0 copy-start.2
  362.5 5.8 slice-start
  363.7 4.6 slice-start.1
  363.7 4.6 copy-start.15
  363.7 4.6 copy-start.16
  369.4 1.1 copy-start.6
  370.5 1.1 copy-start.7
  371.6 1.5 copy-start.3
  371.6 1.5 copy-start.18
  377.6 3.4 copy-start.23
  377.6 3.4 copy-start.26
  377.6 3.4 copy-start.30
  378.7 2.3 copy-start.19
  381.1 3.8 copy-start.4
  401.3 232.9 %reduce-scatter.13.cloned.1.call-start = ((), (), s32[]{:S(2)}) async-start(), calls=%async_computation.7 | async-start | bytes 442368
  401.6 6.6 copy-start.9
  408.1 239.0 %reduce-scatter.17.cloned.1.call-start = ((), (), s32[]{:S(2)}) async-start(), calls=%async_computation.9 | async-start | bytes 442368
  410.4 257.1 %all-gather.9.cloned.1.call-start = ((), (), s32[]{:S(2)}) async-start(), calls=%async_computation.5 | async-start | bytes 3072000 | tf_op jit(solution)/shard_map/all_gather | solution.py:565
  410.4 2.7 copy-start.33
  413.0 284.7 %reduce-scatter.15.cloned.1.call-start = ((), (), s32[]{:S(2)}) async-start(), calls=%async_computation.8 | async-start | bytes 1474560
  602.3 116.0 %reduce-scatter.11.cloned.1.call-start = ((), (), s32[]{:S(2)}) async-start(), calls=%async_computation.6 | async-start | bytes 40960 | tf_op jit(solution)/shard_map/reduce_scatter | solution.py:570
  602.3 3.7 copy-start.10
  709.8 8.5 %copy-start.21 = (f32[16,384]{1,0:T(8,128)S(1)}, f32[16,384]{1,0:T(8,128)}, u32[]{:S(2)}) copy-start(f32[16,384]{1,0:T(8,128)} %get-tuple-element.128) | copy-start | bytes 73732
  709.8 9.1 %copy-start.1 = (bf16[8,197,768]{2,0,1:T(8,128)(2,1)S(1)}, bf16[8,197,768]{2,0,1:T(8,128)(2,1)}, u32[]{:S(2)}) copy-start(bf16[8,197,768]{2,0,1:T(8,128)(2,1)} %param.17) | copy-start | bytes 7262212
Sparse Core Ops, SparseCore 0:
  31.2 38.2 all-gather.6
  401.4 137.2 all-reduce.2
  542.6 33.8 reduce-scatter.12
  579.7 33.8 reduce-scatter.16
  615.1 52.2 all-gather.8
  669.7 27.9 reduce-scatter.14
  700.6 17.6 reduce-scatter.10
